TPU v7x, 256 devices: a whole 4x4x8 slice. The times are simulated.
256 devices in a mesh: dp: 2 (over core), seq: 32 (over y, z), head: 4 (over x).
Axes of the slice: x: 4, y: 4, z: 8, core: 2. Of those that a mesh axis runs over, the one named last changes fastest.
Arguments:
- inputs: bfloat16 [2, 8192, 8192], P('dp', 'seq', 'head'), may hold values from -6 to 6
- proj_b: bfloat16 [2, 8192, 128], P('dp', 'seq'), may hold values from -2 to 2
- proj_c: bfloat16 [2, 8192, 128], P('dp', 'seq'), may hold values from -2 to 2
- step_size: float32 [2, 128, 8192], P('dp', 'head', 'seq'), may hold values from 0.2 to 2
- decay_rate: float32 [128], P('head'), may hold values from 0 to 0.15
- skip_gain: float32 [128], P('head'), may hold values from 0.5 to 1.5
- doc_lengths: int32 [2, 32], P('dp'), may hold values from 1 to 4096, 8192 in all within a row
- grad_out: bfloat16 [2, 8192, 8192], P('dp', 'seq', 'head'), may hold values from -0.59765625 to 0.59765625
Outputs:
- grad_inputs: bfloat16 [2, 8192, 8192], P('dp', 'seq', 'head')
- grad_b: float32 [2, 8192, 128], P('dp', 'seq')
- grad_c: float32 [2, 8192, 128], P('dp', 'seq')
- grad_step: float32 [2, 128, 8192], P('dp', 'head', 'seq')
- grad_rate: float32 [128], P('head')
- grad_skip: float32 [128], P('head')
Inputs may be any that keep to these rules, and one draw needn't show every extreme that they name: `doc_lengths`: each row holds the 32 lengths of one sequence's documents, summing to 8192; the longest is exactly 4096.
All inputs are finite; a program needn't handle non-finite values.
Results may differ from a plain program's by a relative error of at most 0.0015.
Values sent between devices are 32-bit elements; how exact they have to be, the bound alone decides.
A program may use at most 192 MiB of HBM per device.

v0:
```python
import jax
import jax.numpy as jnp
from jax import lax
from jax.sharding import PartitionSpec as P

SPAN = 256


exact_mode = lax.Precision.HIGHEST


def entering_2(value, axis, join, neutral, backward):
    count, mine = (lax.axis_size(axis), lax.axis_index(axis))
    pieces = jax.tree.map(lambda part: lax.all_gather(part, axis), value)
    if backward:
        pieces = jax.tree.map(lambda part: part[::-1], pieces)
        mine = count - 1 - mine
    running = jax.tree.map(
        lambda part, zero: jnp.full_like(part, 0) + jnp.asarray(zero, part.dtype), value, neutral
    )

    def hop(position, running):
        longer = join(running, jax.tree.map(lambda part: part[position], pieces))
        return jax.tree.map(lambda new, old: jnp.where(position < mine, new, old), longer, running)

    return lax.fori_loop(0, count - 1, hop, running)


def span_step(state, inputs, skip_vec):
    x_span, b_span, c_span, log_span, doc_span, doc_before = inputs
    running = jnp.cumsum(log_span, axis=0).T
    width = doc_span.shape[0]
    order = jnp.arange(width)
    same_doc = (doc_span[:, None] == doc_span[None, :]) & (order[:, None] >= order[None, :])
    log_gap = running[:, :, None] - running[:, None, :]
    decay_mask = jnp.where(same_doc[None], jnp.exp(jnp.where(same_doc[None], log_gap, 0.0)), 0.0)
    scores = jnp.dot(c_span, b_span.T, precision=exact_mode)
    y_local = jnp.einsum("hts,shp->thp", decay_mask * scores[None], x_span, precision=exact_mode)
    entering = jnp.exp(running) * (doc_span == doc_before).astype(jnp.float32)[None, :]
    y_carry = (
        jnp.einsum("tn,hpn->thp", c_span, state, precision=exact_mode) * entering.T[:, :, None]
    )
    y_span = y_local + y_carry + skip_vec[None, :, None] * x_span
    final_doc = doc_span[-1]
    leaving = (
        jnp.exp(running[:, -1:] - running) * (doc_span == final_doc).astype(jnp.float32)[None, :]
    )
    carried = jnp.exp(running[:, -1]) * (final_doc == doc_before).astype(jnp.float32)
    added = jnp.einsum("hs,sn,shp->hpn", leaving, b_span, x_span, precision=exact_mode)
    new_state = carried[:, None, None] * state + added
    return (new_state, y_span)


def run_spans(x_tokens, b_tokens, c_tokens, log_decay, doc_ids, doc_before, state, skip_vec, span):
    count = x_tokens.shape[0] // span
    befores = jnp.concatenate([doc_before, doc_ids[span - 1 :: span][:-1]])

    def split(array):
        return array.reshape((count, span) + array.shape[1:])

    def advance(carry, inputs):
        return span_step(carry, inputs, skip_vec)

    final_state, outputs = lax.scan(
        advance,
        state,
        (
            split(x_tokens),
            split(b_tokens),
            split(c_tokens),
            split(log_decay),
            split(doc_ids),
            befores,
        ),
    )
    return (outputs.reshape(x_tokens.shape), final_state)


def document_ids(lengths, positions):
    starts = jnp.cumsum(lengths) - lengths
    return jnp.sum((positions[:, None] >= starts[None, :]).astype(jnp.int32), axis=1) - 1


def compose(earlier, later):
    return (earlier[0] * later[0], later[0][:, None, None] * earlier[1] + later[1])


def on_device(inputs, proj_b, proj_c, step_size, decay_rate, skip_gain, doc_lengths, grad_out):
    tokens = inputs.shape[1]
    heads = decay_rate.shape[0]
    head_dim = inputs.shape[2] // heads
    x_tokens = inputs[0].astype(jnp.float32).reshape(tokens, heads, head_dim)
    dy_tokens = grad_out[0].astype(jnp.float32).reshape(tokens, heads, head_dim)
    b_float = proj_b[0].astype(jnp.float32)
    c_float = proj_c[0].astype(jnp.float32)
    step_local = step_size[0]
    anchor = lax.axis_index("seq") * tokens
    positions = anchor + jnp.arange(tokens, dtype=jnp.int32)
    doc_ids = document_ids(doc_lengths[0], positions)
    before_pos = jnp.reshape(anchor - 1, (1,))
    doc_before = jnp.where(before_pos < 0, -1, document_ids(doc_lengths[0], before_pos))
    running = jnp.cumsum(-(step_local * decay_rate[:, None]), axis=1)
    final_doc = doc_ids[-1]
    through = jnp.exp(running[:, -1]) * (final_doc == doc_before[0]).astype(jnp.float32)
    leaving = (
        jnp.exp(running[:, -1:] - running) * (doc_ids == final_doc).astype(jnp.float32)[None, :]
    )
    local_state = jnp.einsum("hs,sn,shp->hpn", leaving, b_float, x_tokens, precision=exact_mode)
    entering = jnp.exp(running) * (doc_ids == doc_before[0]).astype(jnp.float32)[None, :]
    local_grad = jnp.einsum("ht,tn,thp->hpn", entering, c_float, dy_tokens, precision=exact_mode)
    identity = (jnp.ones((heads,), jnp.float32), jnp.zeros_like(local_state))
    state_in = entering_2((through, local_state), "seq", compose, identity, False)[1]
    grad_state = entering_2((through, local_grad), "seq", compose, identity, True)[1]

    def forward(x_in, b_in, c_in, step_in, rate_in, skip_in):
        log_decay = -(step_in * rate_in[:, None]).T
        return run_spans(x_in, b_in, c_in, log_decay, doc_ids, doc_before, state_in, skip_in, SPAN)

    unused, pullback = jax.vjp(
        forward, x_tokens, b_float, c_float, step_local, decay_rate, skip_gain
    )
    grad_x, grad_bpart, grad_cpart, grad_steps, rate_part, skip_part = pullback(
        (dy_tokens, grad_state)
    )
    shared_b, shared_c = lax.psum((grad_bpart, grad_cpart), "head")
    rate_sum, skip_sum = lax.psum((rate_part, skip_part), ("dp", "seq"))
    grad_inputs = grad_x.reshape(1, tokens, heads * head_dim).astype(jnp.bfloat16)
    return (grad_inputs, shared_b[None], shared_c[None], grad_steps[None], rate_sum, skip_sum)


def solution(mesh):
    in_specs = (
        P("dp", "seq", "head"),
        P("dp", "seq", None),
        P("dp", "seq", None),
        P("dp", "head", "seq"),
        P("head"),
        P("head"),
        P("dp", None),
        P("dp", "seq", "head"),
    )
    out_specs = (
        P("dp", "seq", "head"),
        P("dp", "seq", None),
        P("dp", "seq", None),
        P("dp", "head", "seq"),
        P("head"),
        P("head"),
    )
    return jax.shard_map(
        on_device, mesh=mesh, in_specs=in_specs, out_specs=out_specs, check_vma=False
    )
```

profile of v0, /device:TPU:8, one launch (start us, length us, event | category | flops | bytes accessed | tf_op | source)
XLA Modules:
  0.0 730.2 jit_solution(11833640831729299938)
XLA Ops:
  15.6 1.5 copy.111
  18.0 2.2 fusion.20
  21.1 2.1 fusion.14
  25.5 66.4 %all-reduce.2 = f32[1024]{0:T(1024)S(1)} all-reduce(f32[1024]{0:T(1024)S(1)} %dynamic-update-slice), channel_id=2, replica_groups=mesh['dp'=2,'seq'=32,'head'=4] {'seq'}, use_global_device_ids=true, to_apply=%add.2 | all-reduce | flops 1024 | bytes 8192
  93.4 7.2 fusion.7
  100.6 1.5 copy.116
  102.1 1.5 copy.117
  103.7 152.5 %all-gather.8.cloned.1.call-done = f32[1024,64,128]{2,1,0:T(8,128)} async-done(((f32[32,64,128]{2,1,0:T(8,128)}), f32[1024,64,128]{2,1,0:T(8,128)}) %all-gather.8.cloned.1.call-update) | async-done | bytes 33554448 | tf_op jit(solution)/shard_map/all_gather | solution.py:14
  256.1 47.2 %while.21 = (s32[]{:T(128)}, f32[32,64,128]{2,1,0:T(8,128)S(1)}, s32[]{:T(128)}, f32[32,32]{1,0:T(8,128)S(1)}, f32[32,32,64,128]{3,2,1,0:T(8,128)}, /*index=5*/s32[]{:T(128)}, s32[]{:T(128)}) while((s32[]{:T(128)}, f32[32,64,128]{2,1,0:T(8,128)S(1)}, s32[]{:T(128)}, f32[32,32]{1,0:T(8,128)S(1)}, f32[32,32,64,128]{3,2,1,0:T(8,128)}, ...), condition=%wide.region_12.13_spmd.clone, body=%wide.region_11.12_spmd.clone.sunk | while | flops 1048580 | bytes 3146217 | solution.py:26
  268.2 1.6 fusion.67
  269.8 1.6 fusion.67
  271.4 1.6 fusion.67
  277.6 1.5 fusion.67
  289.7 1.5 fusion.67
  291.2 1.5 fusion.67
  292.8 1.5 fusion.67
  303.3 185.8 %all-gather.6.cloned.1.call-done = f32[1024,64,128]{2,1,0:T(8,128)} async-done(((f32[32,64,128]{2,1,0:T(8,128)}), f32[1024,64,128]{2,1,0:T(8,128)}) %all-gather.6.cloned.1.call-update) | async-done | bytes 33554448 | tf_op jit(solution)/shard_map/all_gather | solution.py:14
  489.1 23.3 %rev.7 = f32[32,32,64,128]{3,2,1,0:T(8,128)} reverse(f32[32,32,64,128]{3,2,1,0:T(8,128)} %bitcast.146), dimensions={0} | reverse | bytes 67108864 | tf_op jit(solution)/shard_map/rev | solution.py:16
  512.4 46.6 %while.20 = (s32[]{:T(128)}, f32[32,64,128]{2,1,0:T(8,128)S(1)}, s32[]{:T(128)}, f32[32,32]{1,0:T(8,128)S(1)}, f32[32,32,64,128]{3,2,1,0:T(8,128)}, /*index=5*/s32[]{:T(128)}, s32[]{:T(128)}) while((s32[]{:T(128)}, f32[32,64,128]{2,1,0:T(8,128)S(1)}, s32[]{:T(128)}, f32[32,32]{1,0:T(8,128)S(1)}, f32[32,32,64,128]{3,2,1,0:T(8,128)}, ...), condition=%wide.region_6.7_spmd.clone, body=%wide.region_5.6_spmd.clone.sunk | while | flops 1048580 | bytes 3146217 | solution.py:26
  558.9 3.0 fusion.21
  563.1 1.6 fusion.18
  565.6 1.5 copy.115
  567.9 2.0 fusion.33
  570.8 2.7 reduce-window.41
  574.6 1.6 fusion.13
  577.0 4.1 convolution_bitcast_fusion
  581.1 1.7 copy.110
  582.8 4.2 fusion.24
  589.1 7.2 fusion.17
  598.2 121.7 %all-reduce.3 = (f32[32]{0:T(128)}, f32[32]{0:T(128)}) all-reduce(f32[32]{0:T(128)S(1)} %fusion.45, f32[32]{0:T(128)S(1)} %reduce_sum.149), channel_id=1, replica_groups=mesh['dp'=2,'seq'=32,'head'=4] {'dp','seq'}, use_global_device_ids=true, to_apply=%region_22.23 | all-reduce | flops 64 | bytes 512 | tf_op jit(solution)/shard_map/psum | solution.py:126
  720.6 1.6 copy.156
  722.1 1.6 copy.157
  (218 shorter events, 102.3 us)
Async XLA Ops:
  7.2 10.8 %copy-start = (bf16[1,256,128]{2,1,0:T(8,128)(2,1)S(1)}, bf16[1,256,128]{2,1,0:T(8,128)(2,1)}, u32[]{:S(2)}) copy-start(bf16[1,256,128]{2,1,0:T(8,128)(2,1)} %param.13) | copy-start | bytes 196612
  7.2 249.0 %all-gather.8.cloned.1.call-start = ((), (), s32[]{:S(2)}) async-start(), calls=%async_computation.1 | async-start | bytes 34603008 | tf_op jit(solution)/shard_map/all_gather | solution.py:14
  17.1 3.3 copy-start.5
  20.1 0.9 copy-start.4
  20.2 468.9 %all-gather.6.cloned.1.call-start = ((), (), s32[]{:S(2)}) async-start(), calls=%async_computation | async-start | bytes 34603008 | tf_op jit(solution)/shard_map/all_gather | solution.py:14
  21.0 2.3 copy-start.1
  21.0 3.0 copy-start.18
  21.1 4.2 copy-start.17
  21.1 70.9 %copy-start.10 = (f32[1,32,256]{2,1,0:T(8,128)S(1)}, f32[1,32,256]{2,1,0:T(8,128)}, u32[]{:S(2)}) copy-start(f32[1,32,256]{2,1,0:T(8,128)} %param.15) | copy-start | bytes 98308
  21.1 70.9 %copy-start.16 = (f32[32]{0:T(128)S(1)}, f32[32]{0:T(128)}, u32[]{:S(2)}) copy-start(f32[32]{0:T(128)} %param.16) | copy-start | bytes 388
  23.3 697.3 %all-reduce.7.cloned.1.call-start = ((), (), s32[]{:S(2)}) async-start(), calls=%async_computation.2 | async-start | bytes 524288 | tf_op jit(solution)/shard_map/psum | solution.py:125
  92.9 7.7 %copy-start.13 = (f32[32,256]{1,0:T(8,128)}, f32[32,256]{1,0:T(8,128)S(1)}, u32[]{:S(2)}) copy-start(f32[32,256]{1,0:T(8,128)S(1)} %copy_bitcast_fusion) | copy-start | bytes 98308
  93.2 7.5 %copy-start.15 = (pred[256,256]{1,0:T(8,128)(4,1)}, pred[256,256]{1,0:T(8,128)(4,1)S(1)}, u32[]{:S(2)}) copy-start(pred[256,256]{1,0:T(8,128)(4,1)S(1)} %fusion.30) | copy-start | bytes 196612
  93.4 7.3 copy-start.12
  561.9 1.2 copy-start.2
  573.5 2.8 copy-start.8
  577.0 10.1 %copy-start.6 = (f32[256,256]{1,0:T(8,128)S(1)}, f32[256,256]{1,0:T(8,128)}, u32[]{:S(2)}) copy-start(f32[256,256]{1,0:T(8,128)} %get-tuple-element.549) | copy-start | bytes 786436
  581.1 8.0 %copy-start.3 = (bf16[1,256,2048]{1,2,0:T(8,128)(2,1)S(1)}, bf16[1,256,2048]{1,2,0:T(8,128)(2,1)}, u32[]{:S(2)}) copy-start(bf16[1,256,2048]{1,2,0:T(8,128)(2,1)} %copy-done.1) | copy-start | bytes 3145732
  582.8 4.3 copy-start.7
  589.0 7.3 copy-start.9
  589.1 7.3 copy-start.11
  589.1 7.6 %copy-start.14 = (f32[32,2,128]{2,0,1:T(8,128)S(1)}, f32[32,2,128]{2,0,1:T(8,128)}, u32[]{:S(2)}) copy-start(f32[32,2,128]{2,0,1:T(8,128)} %add_negate_fusion) | copy-start | bytes 98308
Sparse Core Ops, SparseCore 0:
  20.3 235.8 all-gather.7
  258.7 230.3 all-gather.5
  589.2 45.1 all-reduce.6
where the time goes:
time: 741 us; the launch traced here: 730 us
  waiting for transfers between devices  338 us (46%)
  blocking collectives  188 us (25%)
  other arithmetic  108 us (15%)
  local copies, waits for them, and re-layouts  43.6 us (6%)
  matrix products  33.9 us (5%)
  between operations  16.8 us (2%)
    all_gather x2, waiting for transfers between devices, entering_2(): pieces = jax.tree.map(lambda part: lax.all_gather(part, axis), value)  338 us
    psum x1, blocking collectives, on_device(): rate_sum, skip_sum = lax.psum((rate_part, skip_part), ('dp', 'seq'))  122 us
    select_n x62, other arithmetic, hop(): jnp.where(position < mine, new, old)  91.2 us
    unnamed x1, blocking collectives  66.4 us
    rev x2, local copies, waits for them, and re-layouts, entering_2(): pieces = jax.tree.map(lambda part: part[::-1], pieces)  23.3 us
  transfers between devices with their start and end apart: 3, of which 2 were waited for; matrix products, arithmetic and copies ran while one was open for 10% of the time, Pallas kernels for 0%

commit v1 on v0

v1 whole, which is shorter than its diff:
```python
import jax
import jax.numpy as jnp
from jax import lax
from jax.experimental import pallas as pl
from jax.experimental.pallas import tpu as pltpu
from jax.sharding import PartitionSpec as P

F32 = jnp.float32
BF16 = jnp.bfloat16
MESH = pl.DeviceIdType.MESH

ROWS = 4
RING = 8
SEQ = ROWS * RING
HEADS_AX = 4
TOK = 256
HEADS = 32
HEAD_DIM = 64
STATE = 128
FEAT = HEADS * HEAD_DIM
WIDE = 256
GROUPS = FEAT // WIDE
SLICES = 4 * GROUPS
HALF = STATE // 2
MSG = 2 * HALF + 8
LAG = 3


def nn(a, b):
    return lax.dot_general(a, b, (((1,), (0,)), ((), ())), preferred_element_type=F32)


def nt(a, b):
    return lax.dot_general(a, b, (((1,), (1,)), ((), ())), preferred_element_type=F32)


def split2(value):
    high = value.astype(BF16)
    return high, (value - high.astype(F32)).astype(BF16)


def split3(value):
    high = value.astype(BF16)
    rest = value - high.astype(F32)
    middle = rest.astype(BF16)
    return high, middle, (rest - middle.astype(F32)).astype(BF16)


def iota(shape, dim):
    return lax.broadcasted_iota(jnp.int32, shape, dim)


def kernel(
    x_ref,
    dy_ref,
    b_ref,
    c_ref,
    step_ref,
    rate_ref,
    skip_ref,
    len_ref,
    gx_ref,
    gb_ref,
    gc_ref,
    gs_ref,
    gr_ref,
    gk_ref,
    xh_ref,
    xl_ref,
    dyh_ref,
    dyl_ref,
    em_ref,
    dx_ref,
    yl_ref,
    ob_ref,
    rt_ref,
    sm_ref,
    smt_ref,
    ds_ref,
    cb_ref,
    cbt_ref,
    g_ref,
    th_ref,
    skx_ref,
    sk_ref,
    rc_ref,
    l_ref,
    ld_ref,
    recv_p,
    recv_m,
    send_p,
    send_m,
    cin_s,
    cin_d,
    ysend_s,
    ysend_d,
    sp_ref,
    dp_ref,
    acc_ref,
    part_ref,
    rs_ref,
    sum_ref,
    full_ref,
    vec_ref,
    vdp_ref,
    vec2_ref,
    vz_ref,
    vec3_ref,
    vy_ref,
    p_send,
    p_recv,
    m_send,
    m_recv,
    s_send,
    s_recv,
    d_send,
    d_recv,
    rs_send,
    rs_recv,
    ag_send,
    ag_recv,
    v_send,
    v_recv,
):
    core = lax.axis_index("dp")
    k = lax.axis_index("seq")
    head = lax.axis_index("head")
    y = k // RING
    z = lax.rem(k, RING)
    right = lax.rem(k + 1, SEQ)
    left = lax.rem(k + SEQ - 1, SEQ)
    up = lax.rem(k + RING, SEQ)
    down = lax.rem(k + SEQ - RING, SEQ)

    peers = [{"seq": right}, {"seq": left}, {"dp": 1 - core}]
    peers += [{"seq": y * RING + lax.rem(z + d, RING)} for d in range(1, RING)]
    peers += [{"seq": lax.rem(y + d, ROWS) * RING + z} for d in range(1, ROWS)]
    peers += [{"head": lax.rem(head + d, HEADS_AX)} for d in range(1, HEADS_AX)]
    barrier = pltpu.get_barrier_semaphore()
    for peer in peers:
        pl.semaphore_signal(barrier, inc=1, device_id=peer, device_id_type=MESH)

    lens = len_ref[...].astype(F32)
    docs = lens.shape[1]
    sub, lane = iota((docs, docs), 0), iota((docs, docs), 1)
    lens_col = jnp.sum(jnp.where(sub == lane, lens, 0.0), axis=1, keepdims=True)
    ends_row = jnp.sum(jnp.where(sub <= lane, lens_col, 0.0), axis=0, keepdims=True)
    ends_col = jnp.sum(jnp.where(lane <= sub, lens, 0.0), axis=1, keepdims=True)
    anchor = k * TOK
    pos_c = (anchor + iota((TOK, docs), 0)).astype(F32)
    pos_r = (anchor + iota((docs, TOK), 1)).astype(F32)
    one_r = (anchor + iota((1, docs), 0)).astype(F32)
    doc_c = jnp.sum(jnp.where(ends_row <= pos_c, 1.0, 0.0), axis=1, keepdims=True)
    doc_r = jnp.sum(jnp.where(ends_col <= pos_r, 1.0, 0.0), axis=0, keepdims=True)
    before = jnp.sum(jnp.where(ends_row <= one_r - 1.0, 1.0, 0.0), axis=1, keepdims=True)
    before = jnp.where(one_r[:, :1] < 0.5, -1.0, before)
    last = jnp.sum(jnp.where(ends_row <= one_r + (TOK - 1.0), 1.0, 0.0), axis=1, keepdims=True)
    enter = jnp.where(doc_c == before, 1.0, 0.0)
    leave = jnp.where(doc_c == last, 1.0, 0.0)
    same_end = jnp.where(last == before, 1.0, 0.0)

    bq, cq = b_ref[...], c_ref[...]
    rows, cols = iota((TOK, TOK), 0), iota((TOK, TOK), 1)
    same = doc_c == doc_r
    lower = same & (rows >= cols)
    sm_ref[0], sm_ref[1] = split2(jnp.where(lower, nt(cq, bq), 0.0))
    smt_ref[0], smt_ref[1] = split2(jnp.where(same & (rows <= cols), nt(bq, cq), 0.0))
    cm, bm = cq.astype(F32) * enter, bq.astype(F32) * leave
    cb_ref[0], cb_ref[1] = cm.astype(BF16), bm.astype(BF16)
    cbt_ref[0], cbt_ref[1] = cm.T.astype(BF16), bm.T.astype(BF16)

    hsub, hlane = iota((HEADS, HEADS), 0), iota((HEADS, HEADS), 1)
    rate_col = jnp.sum(jnp.where(hsub == hlane, rate_ref[...], 0.0), axis=1, keepdims=True)
    skip_col = jnp.sum(jnp.where(hsub == hlane, skip_ref[...], 0.0), axis=1, keepdims=True)
    step = step_ref[...]
    tri = jnp.where(rows >= cols, 1.0, 0.0).astype(BF16)
    owner = jnp.where(iota((HEADS, FEAT), 1) // HEAD_DIM == iota((HEADS, FEAT), 0), 1.0, 0.0)
    ob_ref[...] = owner.astype(BF16)
    skx_ref[...] = jnp.sum(owner * skip_col, axis=0, keepdims=True)
    running = sum(nt(tri, part) for part in split3(-(step * rate_col)))
    rt_ref[0], rt_ref[1], rt_ref[2] = split3(running)

    def prepare(i, _):
        at = pl.ds(pl.multiple_of(i * WIDE, WIDE), WIDE)
        ob = ob_ref[:, at]
        rx = nn(rt_ref[0], ob) + nn(rt_ref[1], ob) + nn(rt_ref[2], ob)
        end = rx[TOK - 1 : TOK, :]
        mid = 0.5 * end
        em = jnp.exp(mid - rx)
        em_ref[:, at] = em
        x_f, dy_f = x_ref[:, at].astype(F32), dy_ref[:, at].astype(F32)
        sk_ref[:, at] = jnp.broadcast_to(jnp.sum(x_f * dy_f, axis=0, keepdims=True), (8, WIDE))
        xh, xl = split2(em * x_f)
        dyh, dyl = split2(jnp.exp(rx - mid) * dy_f)
        xh_ref[:, at], xl_ref[:, at], dyh_ref[:, at], dyl_ref[:, at] = xh, xl, dyh, dyl
        g = jnp.exp(mid)
        th = jnp.exp(end) * same_end
        local = g * (nn(cbt_ref[1], xh) + nn(cbt_ref[1], xl))
        local_d = g * (nn(cbt_ref[0], dyh) + nn(cbt_ref[0], dyl))
        for q in range(2):
            cut = slice(q * 128, q * 128 + 128)
            g_ref[2 * i + q] = jnp.broadcast_to(g[:, cut], (8, 128))
            th_ref[2 * i + q] = jnp.broadcast_to(th[:, cut], (8, 128))
            for half in range(2):
                some = slice(half * HALF, half * HALF + HALF)
                l_ref[4 * i + 2 * q + half] = local[some, cut]
                ld_ref[4 * i + 2 * q + half] = local_d[some, cut]
        return 0

    lax.fori_loop(0, GROUPS, prepare, 0)
    rc_ref[...] = jnp.zeros_like(rc_ref)
    ds_ref[...] = jnp.zeros_like(ds_ref)
    pl.semaphore_wait(barrier, len(peers))

    def remote(src, dst, send, recv, device):
        return pltpu.make_async_remote_copy(
            src_ref=src,
            dst_ref=dst,
            send_sem=send,
            recv_sem=recv,
            device_id=device,
            device_id_type=MESH,
        )

    def copy_p(s):
        return remote(send_p.at[s], recv_p.at[s], p_send.at[s], p_recv.at[s], {"seq": right})

    def copy_m(s):
        return remote(send_m.at[s], recv_m.at[s], m_send.at[s], m_recv.at[s], {"seq": left})

    def copy_s(s):
        return remote(ysend_s.at[s], cin_s.at[s], s_send.at[s], s_recv.at[s], {"seq": up})

    def copy_d(s):
        return remote(ysend_d.at[s], cin_d.at[s], d_send.at[s], d_recv.at[s], {"seq": down})

    def chain(s, first, final, edge, copy, recv, send, mine, other):
        @pl.when(first)
        def _():
            recv[s, : 2 * HALF] = jnp.zeros((2 * HALF, 128), F32)
            recv[s, 2 * HALF :] = jnp.ones((8, 128), F32)

        @pl.when(jnp.logical_not(first))
        def _():
            copy(s).wait_recv()

            @pl.when(edge)
            def _():
                recv[s, :HALF] = jnp.zeros((HALF, 128), F32)
                recv[s, 2 * HALF :] = jnp.zeros((8, 128), F32)

        @pl.when(jnp.logical_not(final))
        def _():
            weight = recv[s, 2 * HALF :]
            send[s, HALF : 2 * HALF] = recv[s, HALF : 2 * HALF] + weight[:1] * other[s]
            send[s, 2 * HALF :] = weight * th_ref[s // 2]

        send[s, :HALF] = th_ref[s // 2, 0:1] * recv[s, :HALF] + mine[s]

        @pl.when(jnp.logical_not(final))
        def _():
            copy(s).start()

    def total_s(s):
        return recv_m[s, 2 * HALF : 2 * HALF + 1] * send_p[s, :HALF] + recv_m[s, HALF : 2 * HALF]

    def total_d(s):
        return recv_p[s, 2 * HALF : 2 * HALF + 1] * send_m[s, :HALF] + recv_p[s, HALF : 2 * HALF]

    def finish(s, has_recv, has_send, total, copy, cin, ysend, own, own_weight, dest):
        weight_p = recv_p[s, 2 * HALF : 2 * HALF + 1]
        weight_m = recv_m[s, 2 * HALF : 2 * HALF + 1]

        @pl.when(has_recv)
        def _():
            copy(s).wait_recv()

        @pl.when(jnp.logical_not(has_recv))
        def _():
            cin[s] = jnp.zeros((HALF, 128), F32)

        @pl.when(has_send)
        def _():
            through = weight_p * weight_m * th_ref[s // 2, 0:1]
            ysend[s] = total(s) + through * cin[s]
            copy(s).start()

        weight = weight_p if own_weight else weight_m
        state = own[s, :HALF] + weight * cin[s]
        cin[s] = state
        dest[0, s], dest[1, s] = split2(state * g_ref[s // 2, 0:1])

    def at_slot(slot, which):
        hop = slot // 4
        o = hop if which == 0 else RING - 1 - hop
        group = lax.rem(z - o + RING, RING)
        return group, 4 * group + lax.rem(slot, 4)

    def ywork(tau):
        fresh = (tau >= 16) & (tau < 32)
        for which in range(2):
            group, s = at_slot(jnp.clip(tau, 0, 31), which)

            @pl.when(fresh & (y == ROWS - 1) & (group > 0) & (z >= group))
            def _():
                ysend_s[s] = total_s(s)
                copy_s(s).start()

            @pl.when(fresh & (y == 0) & (z < group))
            def _():
                ysend_d[s] = total_d(s)
                copy_d(s).start()

        for wrap in range(2):
            for which in range(2):
                slot = tau - LAG * (y + wrap)
                group, s = at_slot(jnp.clip(slot, 0, 31), which)
                wraps = (group > 0) & (z >= group)
                mine = wraps if wrap else jnp.logical_not(wraps)

                @pl.when((slot >= 16) & (slot < 32) & mine)
                def _():
                    finish(
                        s,
                        y + wrap > 0,
                        y < ROWS - 1,
                        total_s,
                        copy_s,
                        cin_s,
                        ysend_s,
                        recv_p,
                        True,
                        sp_ref,
                    )

                slot_d = tau - LAG * (ROWS - 1 - y + wrap)
                group_d, s_d = at_slot(jnp.clip(slot_d, 0, 31), which)
                mine_d = z < group_d if wrap else z >= group_d

                @pl.when((slot_d >= 16) & (slot_d < 32) & mine_d)
                def _():
                    finish(
                        s_d,
                        ROWS - 1 - y + wrap > 0,
                        y > 0,
                        total_d,
                        copy_d,
                        cin_d,
                        ysend_d,
                        recv_m,
                        False,
                        dp_ref,
                    )

    def own_heads(i):
        shape = (WIDE, 128)
        hit = iota(shape, 0) // HEAD_DIM + 4 * i == iota(shape, 1)
        return jnp.where(hit, 1.0, 0.0).astype(BF16)

    def add_products(i, at, y_part, dx_part, extra):
        dyp = dyh_ref[:, at].astype(F32) + dyl_ref[:, at].astype(F32)
        xp = xh_ref[:, at].astype(F32) + xl_ref[:, at].astype(F32)
        prod = dyp * y_part - xp * dx_part
        if extra is not None:
            prod = prod + jnp.where(iota((TOK, WIDE), 0) == TOK - 1, extra, 0.0)
        heads = own_heads(i)
        rc_ref[...] += sum(nn(part, heads) for part in split3(prod))

    def local_work(tau):
        i = tau // 4
        at = pl.ds(pl.multiple_of(i * WIDE, WIDE), WIDE)
        turn = lax.rem(tau, 4)

        @pl.when(turn == 0)
        def _():
            yl_ref[...] = (
                nn(sm_ref[0], xh_ref[:, at])
                + nn(sm_ref[0], xl_ref[:, at])
                + nn(sm_ref[1], xh_ref[:, at])
            )

        @pl.when(turn == 1)
        def _():
            dx_ref[:, at] = (
                nn(smt_ref[0], dyh_ref[:, at])
                + nn(smt_ref[0], dyl_ref[:, at])
                + nn(smt_ref[1], dyh_ref[:, at])
            )

        @pl.when(turn == 2)
        def _():
            add_products(i, at, yl_ref[...], dx_ref[:, at], None)

        @pl.when(turn == 3)
        def _():
            ds_ref[...] += (
                nt(dyh_ref[:, at], xh_ref[:, at])
                + nt(dyh_ref[:, at], xl_ref[:, at])
                + nt(dyl_ref[:, at], xh_ref[:, at])
            )

    def slot_body(tau, _):
        @pl.when(tau < 32)
        def _():
            hop = tau // 4
            group, s = at_slot(tau, 0)
            chain(s, hop == 0, hop == RING - 1, k == 0, copy_p, recv_p, send_p, l_ref, ld_ref)
            group, s = at_slot(tau, 1)
            chain(s, hop == 0, hop == RING - 1, k == SEQ - 1, copy_m, recv_m, send_m, ld_ref, l_ref)
            local_work(tau)

        @pl.when(tau >= 16)
        def _():
            ywork(tau)

        return 0

    lax.fori_loop(0, 32 + LAG * ROWS, slot_body, 0)

    def states(ref, part, i):
        a, b, c, d = (ref[part, 4 * i + n] for n in range(4))
        top = jnp.concatenate([a, c], axis=1)
        return jnp.concatenate([top, jnp.concatenate([b, d], axis=1)], axis=0)

    acc_ref[...] = jnp.zeros_like(acc_ref)

    def grads_bc(i, _):
        at = pl.ds(pl.multiple_of(i * WIDE, WIDE), WIDE)
        sh, sl = states(sp_ref, 0, i), states(sp_ref, 1, i)
        dh, dl = states(dp_ref, 0, i), states(dp_ref, 1, i)
        xh, xl, dyh, dyl = xh_ref[:, at], xl_ref[:, at], dyh_ref[:, at], dyl_ref[:, at]
        acc_ref[:, :STATE] += nt(xh, dh) + nt(xl, dh) + nt(xh, dl)
        acc_ref[:, STATE:] += nt(dyh, sh) + nt(dyl, sh) + nt(dyh, sl)
        return 0

    lax.fori_loop(0, GROUPS, grads_bc, 0)
    d_scores = jnp.where(lower, ds_ref[...], 0.0)
    sh, sl = split2(d_scores)
    th, tl = split2(d_scores.T)
    part_ref[:, :STATE] = leave * acc_ref[:, :STATE] + nn(th, cq) + nn(tl, cq)
    part_ref[:, STATE:] = enter * acc_ref[:, STATE:] + nn(sh, bq) + nn(sl, bq)
    quarter = TOK // HEADS_AX

    def copy_rs(d):
        target = lax.rem(head + d, HEADS_AX)
        rows_of = pl.ds(pl.multiple_of(target * quarter, quarter), quarter)
        return remote(
            part_ref.at[rows_of], rs_ref.at[d], rs_send.at[d], rs_recv.at[d], {"head": target}
        )

    def copy_ag(d):
        target = lax.rem(head + d, HEADS_AX)
        return remote(
            sum_ref, full_ref.at[head], ag_send.at[d], ag_recv.at[d], {"head": target}
        )

    def wait_ag(d):
        source = lax.rem(head + HEADS_AX - d, HEADS_AX)
        target = lax.rem(head + d, HEADS_AX)
        return remote(
            sum_ref, full_ref.at[source], ag_send.at[d], ag_recv.at[d], {"head": target}
        )

    for d in range(1, HEADS_AX):
        copy_rs(d).start()

    def grads_x(i):
        at = pl.ds(pl.multiple_of(i * WIDE, WIDE), WIDE)
        y_part = nn(cb_ref[0], states(sp_ref, 0, i)) + nn(cb_ref[0], states(sp_ref, 1, i))
        dx_part = nn(cb_ref[1], states(dp_ref, 0, i)) + nn(cb_ref[1], states(dp_ref, 1, i))
        ends = []
        for q in range(2):
            total = 0.0
            for half in range(2):
                s = 4 * i + 2 * q + half
                out = th_ref[2 * i + q, 0:1] * cin_s[s] + l_ref[s]
                total = total + jnp.sum(out * cin_d[s], axis=0, keepdims=True)
            ends.append(total)
        add_products(i, at, y_part, dx_part, jnp.concatenate(ends, axis=1))
        whole = em_ref[:, at] * (dx_ref[:, at] + dx_part)
        whole = whole + skx_ref[:, at] * dy_ref[:, at].astype(F32)
        gx_ref[:, at] = whole.astype(BF16)

    def grads_x_step(i, _):
        grads_x(i)
        return 0

    lax.fori_loop(0, GROUPS, grads_x_step, 0)

    mine_rows = pl.ds(pl.multiple_of(head * quarter, quarter), quarter)
    for d in range(1, HEADS_AX):
        copy_rs(d).wait()
    sum_ref[...] = part_ref[mine_rows] + rs_ref[1] + rs_ref[2] + rs_ref[3]
    full_ref[head] = sum_ref[...]
    for d in range(1, HEADS_AX):
        copy_ag(d).start()

    dl = sum(nn(part[:HEADS], tri) for part in split3(rc_ref[...].T))
    gs_ref[...] = -(rate_col * dl)
    rate_part = -jnp.sum(step * dl, axis=1, keepdims=True)
    skip_part = sum(nt(ob_ref[...], part) for part in split3(sk_ref[...]))[:, :1]
    diag = iota((HEADS, 128), 0) == iota((HEADS, 128), 1)
    rate_row = jnp.sum(jnp.where(diag, rate_part, 0.0), axis=0, keepdims=True)
    skip_row = jnp.sum(jnp.where(diag, skip_part, 0.0), axis=0, keepdims=True)
    first = iota((8, 128), 0)
    vec_ref[...] = jnp.where(first == 0, rate_row, jnp.where(first == 1, skip_row, 0.0))

    swap = remote(vec_ref, vdp_ref, v_send.at[0], v_recv.at[0], {"dp": 1 - core})
    swap.start()
    swap.wait()
    vec2_ref[...] = vec_ref[...] + vdp_ref[...]
    vz_ref[z] = vec2_ref[...]

    def copy_z(d, slot):
        target = y * RING + lax.rem(z + d, RING)
        return remote(vec2_ref, vz_ref.at[slot], v_send.at[d], v_recv.at[d], {"seq": target})

    for d in range(1, RING):
        copy_z(d, z).start()
    for d in range(1, RING):
        copy_z(d, lax.rem(z + RING - d, RING)).wait()
    vec3_ref[...] = sum(vz_ref[n] for n in range(RING))
    vy_ref[y] = vec3_ref[...]

    def copy_y(d, slot):
        target = lax.rem(y + d, ROWS) * RING + z
        n = RING + d
        return remote(vec3_ref, vy_ref.at[slot], v_send.at[n], v_recv.at[n], {"seq": target})

    for d in range(1, ROWS):
        copy_y(d, y).start()
    for d in range(1, ROWS):
        copy_y(d, lax.rem(y + ROWS - d, ROWS)).wait()
    whole_vec = sum(vy_ref[n] for n in range(ROWS))
    gr_ref[...] = whole_vec[0:1, :HEADS]
    gk_ref[...] = whole_vec[1:2, :HEADS]

    for d in range(1, HEADS_AX):
        wait_ag(d).wait()
    for n in range(HEADS_AX):
        gb_ref[n * quarter : (n + 1) * quarter] = full_ref[n, :, :STATE]
        gc_ref[n * quarter : (n + 1) * quarter] = full_ref[n, :, STATE:]

    def drain(s, _):
        group = s // 4
        o = lax.rem(z - group + RING, RING)

        @pl.when(o < RING - 1)
        def _():
            copy_p(s).wait_send()

        @pl.when(o > 0)
        def _():
            copy_m(s).wait_send()

        @pl.when((y < ROWS - 1) | ((group > 0) & (z >= group)))
        def _():
            copy_s(s).wait_send()

        @pl.when((y > 0) | (z < group))
        def _():
            copy_d(s).wait_send()

        return 0

    lax.fori_loop(0, SLICES, drain, 0)


def on_device(inputs, proj_b, proj_c, step_size, decay_rate, skip_gain, doc_lengths, grad_out):
    vmem = pl.BlockSpec(memory_space=pltpu.VMEM)
    state = pltpu.VMEM((SLICES, HALF, 128), F32)
    message = pltpu.VMEM((SLICES, MSG, 128), F32)
    pair = pltpu.VMEM((2, SLICES, HALF, 128), BF16)
    sems = pltpu.SemaphoreType.DMA((SLICES,))
    tile = pltpu.VMEM((8, 128), F32)
    quarter = TOK // HEADS_AX
    scratch = [
        pltpu.VMEM((TOK, FEAT), BF16),
        pltpu.VMEM((TOK, FEAT), BF16),
        pltpu.VMEM((TOK, FEAT), BF16),
        pltpu.VMEM((TOK, FEAT), BF16),
        pltpu.VMEM((TOK, FEAT), F32),
        pltpu.VMEM((TOK, FEAT), F32),
        pltpu.VMEM((TOK, WIDE), F32),
        pltpu.VMEM((HEADS, FEAT), BF16),
        pltpu.VMEM((3, TOK, HEADS), BF16),
        pltpu.VMEM((2, TOK, TOK), BF16),
        pltpu.VMEM((2, TOK, TOK), BF16),
        pltpu.VMEM((TOK, TOK), F32),
        pltpu.VMEM((2, TOK, STATE), BF16),
        pltpu.VMEM((2, STATE, TOK), BF16),
        pltpu.VMEM((FEAT // 128, 8, 128), F32),
        pltpu.VMEM((FEAT // 128, 8, 128), F32),
        pltpu.VMEM((1, FEAT), F32),
        pltpu.VMEM((8, FEAT), F32),
        pltpu.VMEM((TOK, 128), F32),
        state,
        state,
        message,
        message,
        message,
        message,
        state,
        state,
        state,
        state,
        pair,
        pair,
        pltpu.VMEM((TOK, 2 * STATE), F32),
        pltpu.VMEM((TOK, 2 * STATE), F32),
        pltpu.VMEM((HEADS_AX, quarter, 2 * STATE), F32),
        pltpu.VMEM((quarter, 2 * STATE), F32),
        pltpu.VMEM((HEADS_AX, quarter, 2 * STATE), F32),
        tile,
        tile,
        tile,
        pltpu.VMEM((RING, 8, 128), F32),
        tile,
        pltpu.VMEM((ROWS, 8, 128), F32),
        sems,
        sems,
        sems,
        sems,
        sems,
        sems,
        sems,
        sems,
        pltpu.SemaphoreType.DMA((HEADS_AX,)),
        pltpu.SemaphoreType.DMA((HEADS_AX,)),
        pltpu.SemaphoreType.DMA((HEADS_AX,)),
        pltpu.SemaphoreType.DMA((HEADS_AX,)),
        pltpu.SemaphoreType.DMA((RING + ROWS,)),
        pltpu.SemaphoreType.DMA((RING + ROWS,)),
    ]
    grad_x, grad_b, grad_c, grad_step, grad_rate, grad_skip = pl.pallas_call(
        kernel,
        out_shape=(
            jax.ShapeDtypeStruct((TOK, FEAT), BF16),
            jax.ShapeDtypeStruct((TOK, STATE), F32),
            jax.ShapeDtypeStruct((TOK, STATE), F32),
            jax.ShapeDtypeStruct((HEADS, TOK), F32),
            jax.ShapeDtypeStruct((1, HEADS), F32),
            jax.ShapeDtypeStruct((1, HEADS), F32),
        ),
        in_specs=[vmem] * 8,
        out_specs=(vmem,) * 6,
        scratch_shapes=scratch,
        compiler_params=pltpu.CompilerParams(
            collective_id=0, has_side_effects=True, vmem_limit_bytes=56 << 20
        ),
    )(
        inputs[0],
        grad_out[0],
        proj_b[0],
        proj_c[0],
        step_size[0],
        decay_rate[None],
        skip_gain[None],
        doc_lengths,
    )
    return (
        grad_x[None],
        grad_b[None],
        grad_c[None],
        grad_step[None],
        grad_rate[0],
        grad_skip[0],
    )


def solution(mesh):
    in_specs = (
        P("dp", "seq", "head"),
        P("dp", "seq", None),
        P("dp", "seq", None),
        P("dp", "head", "seq"),
        P("head"),
        P("head"),
        P("dp", None),
        P("dp", "seq", "head"),
    )
    out_specs = (
        P("dp", "seq", "head"),
        P("dp", "seq", None),
        P("dp", "seq", None),
        P("dp", "head", "seq"),
        P("head"),
        P("head"),
    )
    return jax.shard_map(
        on_device, mesh=mesh, in_specs=in_specs, out_specs=out_specs, check_vma=False
    )
```

time: 741 us -> 120 us (0.16); the launches traced: 730 us -> 119 us
  waiting for transfers between devices: 338 us -> 0 us
  blocking collectives: 188 us -> 0 us
  Pallas kernels: 0 us -> 113 us
  other arithmetic: 108 us -> 0 us
  local copies, waits for them, and re-layouts: 43.6 us -> 5.85 us
  matrix products: 33.9 us -> 0 us
  between operations: 16.8 us -> 0.66 us
    all_gather x2 -> x0, waiting for transfers between devices: 338 us -> none  [entering_2(): pieces = jax.tree.map(lambda part: lax.all_gather(part, axis), value)]
    psum x1 -> x0, blocking collectives: 122 us -> none  [on_device(): rate_sum, skip_sum = lax.psum((rate_part, skip_part), ('dp', 'seq'))]
    pallas_call x0 -> x1, Pallas kernels: none -> 113 us  [on_device(): pl.pallas_call(kernel, out_shape=(jax.ShapeDtypeStruct((TOK, FEAT), BF16)...]
    select_n x62 -> x0, other arithmetic: 91.2 us -> none  [hop(): jnp.where(position < mine, new, old)]
    unnamed x1 -> x0, blocking collectives: 66.4 us -> none
    dot_general x11 -> x0, matrix products: 33.9 us -> none  [the longest x2 14.5 us: span_step(): jnp.einsum('hts,shp->thp', decay_mask * scores[None], x_span, precision=e...]
    rev x2 -> x0, local copies, waits for them, and re-layouts: 23.3 us -> none  [entering_2(): pieces = jax.tree.map(lambda part: part[::-1], pieces)]
  transfers between devices with their start and end apart: 3 -> 0, of which waited for: 2 -> 0; matrix products, arithmetic and copies ran while one was open for 10% -> 0% of each run, Pallas kernels for 0% -> 0%
where the time goes in v1:
time: 120 us; the launch traced here: 119 us
  Pallas kernels  113 us (94%)
  local copies, waits for them, and re-layouts  5.85 us (5%)
    pallas_call x1, Pallas kernels, on_device(): pl.pallas_call(kernel, out_shape=(jax.ShapeDtypeStruct((TOK, FEAT), BF16)...  113 us
    unnamed x16, local copies, waits for them, and re-layouts  5.85 us

profile of v1, /device:TPU:8, one launch (start us, length us, event | category | flops | bytes accessed | tf_op | source)
XLA Modules:
  0.0 119.1 jit_solution(5055559147283685398)
XLA Ops:
  0.6 112.6 %shard_map.127 = (bf16[256,2048]{1,0:T(8,128)(2,1)}, f32[256,128]{1,0:T(8,128)}, f32[256,128]{1,0:T(8,128)}, f32[32,256]{1,0:T(8,128)}, f32[1,32]{1,0:T(1,128)}, /*index=5*/f32[1,32]{1,0:T(1,128)}) custom-call(bf16[256,2048]{1,0:T(8,128)(2,1)} %bitcast.13, bf16[256,2048]{1,0:T(8,128)(2,1)} %bitcast.14, bf16[256,128]{1,0:T(8,128)(2,1)} %bitcast.18, ...), custom_call_target="tpu_custom_call" | custom-call | tf_op jit(solution)/shard_map/pallas_call | solution.py:635
  113.2 0.0 copy-start.1
  113.2 2.3 %copy.20 = bf16[1,256,2048]{2,1,0:T(8,128)(2,1)} copy(bf16[1,256,2048]{2,1,0:T(8,128)(2,1)} %bitcast.15) | data formatting | bytes 2097152
  115.6 0.0 copy-done.1
  115.6 0.0 copy-start
  115.6 0.7 copy.21
  116.2 0.3 copy-done
  116.5 0.0 copy-start.2
  116.5 0.7 copy.22
  117.2 0.1 copy-done.2
  117.3 0.0 copy-start.4
  117.3 0.6 copy.23
  117.9 0.0 copy-done.4
  117.9 0.0 copy-start.3
  117.9 0.5 copy.24
  118.4 0.2 copy-done.3
  118.6 0.5 copy.25
Async XLA Ops:
  113.2 2.4 %copy-start.1 = (f32[256,128]{1,0:T(8,128)S(1)}, f32[256,128]{1,0:T(8,128)}, u32[]{:S(2)}) copy-start(f32[256,128]{1,0:T(8,128)} %get-tuple-element.13) | copy-start | bytes 393220
  115.6 1.0 copy-start
  116.5 0.8 copy-start.2
  117.3 0.6 copy-start.4
  117.9 0.7 copy-start.3

commit v2 on v1

v2 whole, which is shorter than its diff:
```python
import jax
import jax.numpy as jnp
from jax import lax
from jax.experimental import pallas as pl
from jax.experimental.pallas import tpu as pltpu
from jax.sharding import PartitionSpec as P

F32 = jnp.float32
BF16 = jnp.bfloat16
MESH = pl.DeviceIdType.MESH

ROWS = 4
RING = 8
SEQ = ROWS * RING
HEADS_AX = 4
TOK = 256
HEADS = 32
HEAD_DIM = 64
STATE = 128
FEAT = HEADS * HEAD_DIM
WIDE = 256
GROUPS = FEAT // WIDE
PIECES = 2
PER = 2 * PIECES
SLICES = PER * GROUPS
HALF = STATE // PIECES
LATE = SLICES // 2
HOP = 3 * PIECES // 2
LAG = 3 * PIECES // 2
DELAY = PER + 2
SLOTS = HOP * (RING - 1) + SLICES
ORDER = (0, 1, 4, 2, 5, 3, 6, 7)


def nn(a, b):
    return lax.dot_general(a, b, (((1,), (0,)), ((), ())), preferred_element_type=F32)


def nt(a, b):
    return lax.dot_general(a, b, (((1,), (1,)), ((), ())), preferred_element_type=F32)


def split2(value):
    high = value.astype(BF16)
    return high, (value - high.astype(F32)).astype(BF16)


def split3(value):
    high = value.astype(BF16)
    rest = value - high.astype(F32)
    middle = rest.astype(BF16)
    return high, middle, (rest - middle.astype(F32)).astype(BF16)


def over(n, size):
    return lax.shift_right_arithmetic(n, jnp.int32(size.bit_length() - 1))


def left_over(n, size):
    return lax.bitwise_and(n, jnp.int32(size - 1))


def iota(shape, dim):
    return lax.broadcasted_iota(jnp.int32, shape, dim)


def kernel(
    x_ref,
    dy_ref,
    b_ref,
    c_ref,
    step_ref,
    rate_ref,
    skip_ref,
    len_ref,
    gx_ref,
    gb_ref,
    gc_ref,
    gs_ref,
    gr_ref,
    gk_ref,
    xh_ref,
    xl_ref,
    dyh_ref,
    dyl_ref,
    em_ref,
    dx_ref,
    yl_ref,
    ob_ref,
    rt_ref,
    sm_ref,
    smt_ref,
    ds_ref,
    cb_ref,
    cbt_ref,
    g_ref,
    th_ref,
    w_ref,
    thz_ref,
    mask_ref,
    skx_ref,
    sk_ref,
    rc_ref,
    l_ref,
    ld_ref,
    recv_p,
    recv_m,
    send_p,
    send_m,
    cin_s,
    cin_d,
    ysend_s,
    ysend_d,
    sp_ref,
    dp_ref,
    acc_ref,
    part_ref,
    rs_ref,
    sum_ref,
    full_ref,
    vec_ref,
    vdp_ref,
    vec2_ref,
    vz_ref,
    vec3_ref,
    vy_ref,
    p_send,
    p_recv,
    m_send,
    m_recv,
    s_send,
    s_recv,
    d_send,
    d_recv,
    rs_send,
    rs_recv,
    ag_send,
    ag_recv,
    v_send,
    v_recv,
    t_send,
    t_recv,
):
    core = lax.axis_index("dp")
    k = lax.axis_index("seq")
    head = lax.axis_index("head")
    y = over(k, RING)
    z = left_over(k, RING)
    right = lax.rem(k + 1, SEQ)
    left = lax.rem(k + SEQ - 1, SEQ)
    up = lax.rem(k + RING, SEQ)
    down = lax.rem(k + SEQ - RING, SEQ)

    peers = [{"dp": 1 - core}]
    peers += [{"seq": y * RING + lax.rem(z + d, RING)} for d in range(1, RING)]
    peers += [{"seq": lax.rem(y + d, ROWS) * RING + z} for d in range(1, ROWS)]
    peers += [{"head": lax.rem(head + d, HEADS_AX)} for d in range(1, HEADS_AX)]
    barrier = pltpu.get_barrier_semaphore()
    for peer in peers:
        pl.semaphore_signal(barrier, inc=1, device_id=peer, device_id_type=MESH)

    lens = len_ref[...].astype(F32)
    docs = lens.shape[1]
    sub, lane = iota((docs, docs), 0), iota((docs, docs), 1)
    lens_col = jnp.sum(jnp.where(sub == lane, lens, 0.0), axis=1, keepdims=True)
    ends_row = jnp.sum(jnp.where(sub <= lane, lens_col, 0.0), axis=0, keepdims=True)
    ends_col = jnp.sum(jnp.where(lane <= sub, lens, 0.0), axis=1, keepdims=True)
    anchor = k * TOK
    pos_c = (anchor + iota((TOK, docs), 0)).astype(F32)
    pos_r = (anchor + iota((docs, TOK), 1)).astype(F32)
    one_r = (anchor + iota((1, docs), 0)).astype(F32)
    doc_c = jnp.sum(jnp.where(ends_row <= pos_c, 1.0, 0.0), axis=1, keepdims=True)
    doc_r = jnp.sum(jnp.where(ends_col <= pos_r, 1.0, 0.0), axis=0, keepdims=True)
    before = jnp.sum(jnp.where(ends_row <= one_r - 1.0, 1.0, 0.0), axis=1, keepdims=True)
    before = jnp.where(one_r[:, :1] < 0.5, -1.0, before)
    last = jnp.sum(jnp.where(ends_row <= one_r + (TOK - 1.0), 1.0, 0.0), axis=1, keepdims=True)
    enter = jnp.where(doc_c == before, 1.0, 0.0)
    leave = jnp.where(doc_c == last, 1.0, 0.0)
    same_end = jnp.where(last == before, 1.0, 0.0)

    bq, cq = b_ref[...], c_ref[...]
    rows, cols = iota((TOK, TOK), 0), iota((TOK, TOK), 1)
    cm, bm = cq.astype(F32) * enter, bq.astype(F32) * leave
    cb_ref[0], cb_ref[1] = cm.astype(BF16), bm.astype(BF16)
    cbt_ref[0], cbt_ref[1] = cm.T.astype(BF16), bm.T.astype(BF16)

    hsub, hlane = iota((HEADS, HEADS), 0), iota((HEADS, HEADS), 1)
    rate_col = jnp.sum(jnp.where(hsub == hlane, rate_ref[...], 0.0), axis=1, keepdims=True)
    skip_col = jnp.sum(jnp.where(hsub == hlane, skip_ref[...], 0.0), axis=1, keepdims=True)
    step = step_ref[...]
    tri = jnp.where(rows >= cols, 1.0, 0.0).astype(BF16)
    owner = jnp.where(iota((HEADS, FEAT), 1) // HEAD_DIM == iota((HEADS, FEAT), 0), 1.0, 0.0)
    ob_ref[...] = owner.astype(BF16)
    skx_ref[...] = jnp.sum(owner * skip_col, axis=0, keepdims=True)
    running = sum(nt(tri, part) for part in split3(-(step * rate_col)))
    rt_ref[0], rt_ref[1], rt_ref[2] = split3(running)

    def remote(src, dst, send, recv, device):
        return pltpu.make_async_remote_copy(
            src_ref=src,
            dst_ref=dst,
            send_sem=send,
            recv_sem=recv,
            device_id=device,
            device_id_type=MESH,
        )

    pl.semaphore_wait(barrier, len(peers))
    passing = jnp.exp(running[TOK - 1 :, :]) * same_end
    wide = jnp.concatenate([passing, jnp.zeros((1, 128 - HEADS), F32)], axis=1)
    thz_ref[z] = jnp.broadcast_to(wide, (8, 128))

    def copy_t(d, slot):
        target = y * RING + lax.rem(z + d, RING)
        return remote(
            thz_ref.at[z], thz_ref.at[slot], t_send.at[d], t_recv.at[d], {"seq": target}
        )

    for d in range(1, RING):
        copy_t(d, z).start()

    def prepare(i):
        at = pl.ds(pl.multiple_of(i * WIDE, WIDE), WIDE)
        ob = ob_ref[:, at]
        rx = nn(rt_ref[0], ob) + nn(rt_ref[1], ob) + nn(rt_ref[2], ob)
        end = rx[TOK - 1 : TOK, :]
        mid = 0.5 * end
        em = jnp.exp(mid - rx)
        em_ref[:, at] = em
        x_f, dy_f = x_ref[:, at].astype(F32), dy_ref[:, at].astype(F32)
        sk_ref[:, at] = jnp.broadcast_to(jnp.sum(x_f * dy_f, axis=0, keepdims=True), (8, WIDE))
        xh, xl = split2(em * x_f)
        dyh, dyl = split2(jnp.exp(rx - mid) * dy_f)
        xh_ref[:, at], xl_ref[:, at], dyh_ref[:, at], dyl_ref[:, at] = xh, xl, dyh, dyl
        g = jnp.exp(mid)
        th = jnp.exp(end) * same_end
        local = g * (nn(cbt_ref[1], xh) + nn(cbt_ref[1], xl))
        local_d = g * (nn(cbt_ref[0], dyh) + nn(cbt_ref[0], dyl))
        for q in range(2):
            cut = slice(q * 128, q * 128 + 128)
            g_ref[2 * i + q] = jnp.broadcast_to(g[:, cut], (8, 128))
            th_ref[2 * i + q] = jnp.broadcast_to(th[:, cut], (8, 128))
            for n in range(PIECES):
                some = slice(n * HALF, n * HALF + HALF)
                l_ref[PER * i + PIECES * q + n] = local[some, cut]
                ld_ref[PER * i + PIECES * q + n] = local_d[some, cut]

    def make_weights():
        for d in range(1, RING):
            copy_t(d, lax.rem(z + RING - d, RING)).wait()
        ones = jnp.ones((8, 128), F32)
        ahead, behind = ones, ones
        for n in range(RING):
            ahead = ahead * jnp.where(n < z, thz_ref[n], ones)
            behind = behind * jnp.where(n > z, thz_ref[n], ones)
        pick = iota((8, 128), 0)
        row = ahead * behind * thz_ref[z]
        table = jnp.where(pick == 0, ahead, jnp.where(pick == 1, behind, row))
        table = sum(nn(part[:, :HEADS], ob_ref[...]) for part in split3(table))
        for n in range(FEAT // 128):
            w_ref[n] = table[:, n * 128 : (n + 1) * 128]

    def make_scores():
        same = doc_c == doc_r
        lower = same & (iota((TOK, TOK), 0) >= iota((TOK, TOK), 1))
        upper = same & (iota((TOK, TOK), 0) <= iota((TOK, TOK), 1))
        sm_ref[0], sm_ref[1] = split2(jnp.where(lower, nt(c_ref[...], b_ref[...]), 0.0))
        smt_ref[0], smt_ref[1] = split2(jnp.where(upper, nt(b_ref[...], c_ref[...]), 0.0))
        mask_ref[...] = jnp.where(lower, 1.0, 0.0)

    w_ref[...] = jnp.ones_like(w_ref)
    acc_ref[...] = jnp.zeros_like(acc_ref)
    rc_ref[...] = jnp.zeros_like(rc_ref)
    ds_ref[...] = jnp.zeros_like(ds_ref)

    def copy_p(s):
        return remote(send_p.at[s], recv_p.at[s], p_send.at[s], p_recv.at[s], {"seq": right})

    def copy_m(s):
        return remote(send_m.at[s], recv_m.at[s], m_send.at[s], m_recv.at[s], {"seq": left})

    def copy_s(s):
        return remote(ysend_s.at[s], cin_s.at[s], s_send.at[s], s_recv.at[s], {"seq": up})

    def copy_d(s):
        return remote(ysend_d.at[s], cin_d.at[s], d_send.at[s], d_recv.at[s], {"seq": down})

    def weights(s):
        fb = over(s, PIECES)
        return th_ref[fb, 0:1], w_ref[fb, 0:1], w_ref[fb, 1:2], w_ref[fb, 2:3]

    def chain(s, first, final, copy, recv, send, mine, other, cin_mine, cin_other, forward):
        th, ahead, behind, _ = weights(s)
        weight = ahead if forward else behind

        @pl.when(first)
        def _():
            recv[s] = jnp.zeros((2 * HALF, 128), F32)

        @pl.when(jnp.logical_not(first))
        def _():
            copy(s).wait_recv()

        @pl.when(s < LATE)
        def _():
            send[s, :HALF] = th * recv[s, :HALF] + mine[s]
            send[s, HALF:] = recv[s, HALF:] + weight * other[s]

        @pl.when(s >= LATE)
        def _():
            send[s, :HALF] = th * (recv[s, :HALF] + weight * cin_mine[s]) + mine[s]
            send[s, HALF:] = recv[s, HALF:] + cin_other[s]

        @pl.when(jnp.logical_not(final))
        def _():
            copy(s).start()

    def pass_on(s, has_recv, has_send, copy, cin, ysend, total):
        @pl.when(has_recv)
        def _():
            copy(s).wait_recv()

        @pl.when(jnp.logical_not(has_recv))
        def _():
            cin[s] = jnp.zeros((HALF, 128), F32)

        @pl.when(has_send)
        def _():
            ysend[s] = total(s) + weights(s)[3] * cin[s]
            copy(s).start()

    def pass_s(s, total):
        pass_on(s, y > 0, y < ROWS - 1, copy_s, cin_s, ysend_s, total)

    def pass_d(s, total):
        pass_on(s, y < ROWS - 1, y > 0, copy_d, cin_d, ysend_d, total)

    def keep(s, state, cin, dest):
        cin[s] = state
        dest[0, s], dest[1, s] = split2(state * g_ref[over(s, PIECES), 0:1])

    def own_heads(i):
        shape = (WIDE, 128)
        hit = iota(shape, 0) // HEAD_DIM + 4 * i == iota(shape, 1)
        return jnp.where(hit, 1.0, 0.0).astype(BF16)

    def add_products(i, at, y_part, dx_part, extra):
        dyp = dyh_ref[:, at].astype(F32) + dyl_ref[:, at].astype(F32)
        xp = xh_ref[:, at].astype(F32) + xl_ref[:, at].astype(F32)
        prod = dyp * y_part - xp * dx_part
        if extra is not None:
            prod = prod + jnp.where(iota((TOK, WIDE), 0) == TOK - 1, extra, 0.0)
        heads = own_heads(i)
        rc_ref[...] += sum(nn(part, heads) for part in split3(prod))

    def local_work(i, turn):
        at = pl.ds(pl.multiple_of(i * WIDE, WIDE), WIDE)

        @pl.when(turn == 0)
        def _():
            yl_ref[...] = (
                nn(sm_ref[0], xh_ref[:, at])
                + nn(sm_ref[0], xl_ref[:, at])
                + nn(sm_ref[1], xh_ref[:, at])
            )

        @pl.when(turn == 1)
        def _():
            dx_ref[:, at] = (
                nn(smt_ref[0], dyh_ref[:, at])
                + nn(smt_ref[0], dyl_ref[:, at])
                + nn(smt_ref[1], dyh_ref[:, at])
            )

        @pl.when(turn == 2)
        def _():
            add_products(i, at, yl_ref[...], dx_ref[:, at], None)

        @pl.when(turn == 3)
        def _():
            ds_ref[...] += (
                nt(dyh_ref[:, at], xh_ref[:, at])
                + nt(dyh_ref[:, at], xl_ref[:, at])
                + nt(dyl_ref[:, at], xh_ref[:, at])
            )

    def states(ref, part, i):
        def column(q):
            some = [ref[part, PER * i + PIECES * q + n] for n in range(PIECES)]
            return jnp.concatenate(some, axis=0)

        return jnp.concatenate([column(0), column(1)], axis=1)

    def grads(i):
        at = pl.ds(pl.multiple_of(i * WIDE, WIDE), WIDE)
        sh, sl = states(sp_ref, 0, i), states(sp_ref, 1, i)
        dh, dl = states(dp_ref, 0, i), states(dp_ref, 1, i)
        xh, xl, dyh, dyl = xh_ref[:, at], xl_ref[:, at], dyh_ref[:, at], dyl_ref[:, at]
        acc_ref[:, :STATE] += nt(xh, dh) + nt(xl, dh) + nt(xh, dl)
        acc_ref[:, STATE:] += nt(dyh, sh) + nt(dyl, sh) + nt(dyh, sl)
        y_part = nn(cb_ref[0], sh) + nn(cb_ref[0], sl)
        dx_part = nn(cb_ref[1], dh) + nn(cb_ref[1], dl)
        ends = []
        for q in range(2):
            total = 0.0
            for n in range(PIECES):
                s = PER * i + PIECES * q + n
                out = th_ref[2 * i + q, 0:1] * cin_s[s] + l_ref[s]
                total = total + jnp.sum(out * cin_d[s], axis=0, keepdims=True)
            ends.append(total)
        add_products(i, at, y_part, dx_part, jnp.concatenate(ends, axis=1))
        whole = em_ref[:, at] * (dx_ref[:, at] + dx_part)
        whole = whole + skx_ref[:, at] * dy_ref[:, at].astype(F32)
        gx_ref[:, at] = whole.astype(BF16)

    far = HOP * jnp.maximum(z, RING - 1 - z)
    hops_s, hops_d = y, ROWS - 1 - y

    def slot_body(number, _):
        tau = number - 1

        @pl.when(tau == 2)
        def _():
            make_weights()

        def at(n, low, high, work):
            @pl.when((n >= low) & (n < high))
            def _():
                work(n)

        def forward(s):
            chain(
                s, z == 0, z == RING - 1, copy_p, recv_p, send_p, l_ref, ld_ref, cin_s, cin_d, True
            )

        def backward(s):
            chain(
                s, z == RING - 1, z == 0, copy_m, recv_m, send_m, ld_ref, l_ref, cin_d, cin_s, False
            )

        at(tau - HOP * z, 0, SLICES, forward)
        at(tau - HOP * (RING - 1 - z), 0, SLICES, backward)

        def early_s(s):
            pass_s(s, lambda s: weights(s)[2] * l_ref[s])

        def early_d(s):
            pass_d(s, lambda s: weights(s)[1] * ld_ref[s])

        at(tau + LATE - DELAY - LAG * hops_s, LATE, SLICES, early_s)
        at(tau + LATE - DELAY - LAG * hops_d, LATE, SLICES, early_d)

        def late_s(s):
            pass_s(s, lambda s: weights(s)[2] * send_p[s, :HALF] + recv_m[s, HALF:])
            keep(s, recv_p[s, :HALF] + weights(s)[1] * cin_s[s], cin_s, sp_ref)

        def late_d(s):
            pass_d(s, lambda s: weights(s)[1] * send_m[s, :HALF] + recv_p[s, HALF:])
            keep(s, recv_m[s, :HALF] + weights(s)[2] * cin_d[s], cin_d, dp_ref)

        at(tau - far - LAG * hops_s, 0, LATE, late_s)
        at(tau - far - LAG * hops_d, 0, LATE, late_d)

        def whole(s):
            _, ahead, behind, _ = weights(s)
            state = recv_p[s, :HALF] + ahead * (cin_s[s] + recv_m[s, HALF:])
            state_d = recv_m[s, :HALF] + behind * (cin_d[s] + recv_p[s, HALF:])
            keep(s, state, cin_s, sp_ref)
            keep(s, state_d, cin_d, dp_ref)

        at(tau - far, LATE, SLICES, whole)

        @pl.when(tau == 0)
        def _():
            make_scores()

        beat = PER // 2
        place = over(tau + beat, beat)

        @pl.when((tau == -1) | ((left_over(tau + beat, beat) == 0) & (place < GROUPS)))
        def _():
            chosen = 0
            for n in range(1, GROUPS):
                chosen = jnp.where((tau >= 0) & (place == n), ORDER[n], chosen)
            prepare(chosen)

        turn = left_over(tau, PER)

        @pl.when((tau >= PER) & (tau < SLICES + PER) & (left_over(turn, PIECES // 2) == 0))
        def _():
            local_work(over(tau, PER) - 1, over(turn, PIECES // 2))

        def both(c, _):
            done = jnp.where(c == 0, tau - far - LAG * jnp.maximum(hops_s, hops_d), tau - far)
            done = done - (PER - 1)
            low = jnp.where(c == 0, 0, LATE)
            high = jnp.where(c == 0, LATE, SLICES)

            @pl.when((done >= low) & (done < high) & (left_over(done, PER) == 0))
            def _():
                grads(over(done, PER))

            return 0

        lax.fori_loop(0, 2, both, 0)
        return 0

    lax.fori_loop(0, SLOTS + 1, slot_body, 0)

    d_scores = jnp.where(mask_ref[...] > 0.5, ds_ref[...], 0.0)
    bq, cq = b_ref[...], c_ref[...]
    sh, sl = split2(d_scores)
    th, tl = split2(d_scores.T)
    part_ref[:, :STATE] = leave * acc_ref[:, :STATE] + nn(th, cq) + nn(tl, cq)
    part_ref[:, STATE:] = enter * acc_ref[:, STATE:] + nn(sh, bq) + nn(sl, bq)
    quarter = TOK // HEADS_AX

    def copy_rs(d):
        target = lax.rem(head + d, HEADS_AX)
        rows_of = pl.ds(pl.multiple_of(target * quarter, quarter), quarter)
        return remote(
            part_ref.at[rows_of], rs_ref.at[d], rs_send.at[d], rs_recv.at[d], {"head": target}
        )

    def copy_ag(d):
        target = lax.rem(head + d, HEADS_AX)
        return remote(
            sum_ref, full_ref.at[head], ag_send.at[d], ag_recv.at[d], {"head": target}
        )

    def wait_ag(d):
        source = lax.rem(head + HEADS_AX - d, HEADS_AX)
        target = lax.rem(head + d, HEADS_AX)
        return remote(
            sum_ref, full_ref.at[source], ag_send.at[d], ag_recv.at[d], {"head": target}
        )

    for d in range(1, HEADS_AX):
        copy_rs(d).start()

    tri = jnp.where(iota((TOK, TOK), 0) >= iota((TOK, TOK), 1), 1.0, 0.0).astype(BF16)
    dl = sum(nn(part[:HEADS], tri) for part in split3(rc_ref[...].T))
    gs_ref[...] = -(rate_col * dl)
    rate_part = -jnp.sum(step * dl, axis=1, keepdims=True)
    skip_part = sum(nt(ob_ref[...], part) for part in split3(sk_ref[...]))[:, :1]
    diag = iota((HEADS, 128), 0) == iota((HEADS, 128), 1)
    rate_row = jnp.sum(jnp.where(diag, rate_part, 0.0), axis=0, keepdims=True)
    skip_row = jnp.sum(jnp.where(diag, skip_part, 0.0), axis=0, keepdims=True)
    first = iota((8, 128), 0)
    vec_ref[...] = jnp.where(first == 0, rate_row, jnp.where(first == 1, skip_row, 0.0))

    swap = remote(vec_ref, vdp_ref, v_send.at[0], v_recv.at[0], {"dp": 1 - core})
    swap.start()
    swap.wait()
    vec2_ref[...] = vec_ref[...] + vdp_ref[...]
    vz_ref[z] = vec2_ref[...]

    def copy_z(d, slot):
        target = y * RING + lax.rem(z + d, RING)
        return remote(vec2_ref, vz_ref.at[slot], v_send.at[d], v_recv.at[d], {"seq": target})

    for d in range(1, RING):
        copy_z(d, z).start()
    mine_rows = pl.ds(pl.multiple_of(head * quarter, quarter), quarter)
    for d in range(1, HEADS_AX):
        copy_rs(d).wait()
    sum_ref[...] = part_ref[mine_rows] + rs_ref[1] + rs_ref[2] + rs_ref[3]
    full_ref[head] = sum_ref[...]
    for d in range(1, HEADS_AX):
        copy_ag(d).start()

    for d in range(1, RING):
        copy_z(d, lax.rem(z + RING - d, RING)).wait()
    vec3_ref[...] = sum(vz_ref[n] for n in range(RING))
    vy_ref[y] = vec3_ref[...]

    def copy_y(d, slot):
        target = lax.rem(y + d, ROWS) * RING + z
        n = RING + d
        return remote(vec3_ref, vy_ref.at[slot], v_send.at[n], v_recv.at[n], {"seq": target})

    for d in range(1, ROWS):
        copy_y(d, y).start()
    for d in range(1, HEADS_AX):
        wait_ag(d).wait()
    for n in range(HEADS_AX):
        gb_ref[n * quarter : (n + 1) * quarter] = full_ref[n, :, :STATE]
        gc_ref[n * quarter : (n + 1) * quarter] = full_ref[n, :, STATE:]
    for d in range(1, ROWS):
        copy_y(d, lax.rem(y + ROWS - d, ROWS)).wait()
    whole_vec = sum(vy_ref[n] for n in range(ROWS))
    gr_ref[...] = whole_vec[0:1, :HEADS]
    gk_ref[...] = whole_vec[1:2, :HEADS]

    def drain(s, _):
        @pl.when(z < RING - 1)
        def _():
            copy_p(s).wait_send()

        @pl.when(z > 0)
        def _():
            copy_m(s).wait_send()

        @pl.when(y < ROWS - 1)
        def _():
            copy_s(s).wait_send()

        @pl.when(y > 0)
        def _():
            copy_d(s).wait_send()

        return 0

    lax.fori_loop(0, SLICES, drain, 0)


def hand_out(*refs):
    count = len(refs) // 2
    for n in range(count):
        refs[count + n][...] = refs[n][...]


def on_device(inputs, proj_b, proj_c, step_size, decay_rate, skip_gain, doc_lengths, grad_out):
    vmem = pl.BlockSpec(memory_space=pltpu.VMEM)
    state = pltpu.VMEM((SLICES, HALF, 128), F32)
    message = pltpu.VMEM((SLICES, 2 * HALF, 128), F32)
    pair = pltpu.VMEM((2, SLICES, HALF, 128), BF16)
    sems = pltpu.SemaphoreType.DMA((SLICES,))
    tile = pltpu.VMEM((8, 128), F32)
    quarter = TOK // HEADS_AX
    scratch = [
        pltpu.VMEM((TOK, FEAT), BF16),
        pltpu.VMEM((TOK, FEAT), BF16),
        pltpu.VMEM((TOK, FEAT), BF16),
        pltpu.VMEM((TOK, FEAT), BF16),
        pltpu.VMEM((TOK, FEAT), F32),
        pltpu.VMEM((TOK, FEAT), F32),
        pltpu.VMEM((TOK, WIDE), F32),
        pltpu.VMEM((HEADS, FEAT), BF16),
        pltpu.VMEM((3, TOK, HEADS), BF16),
        pltpu.VMEM((2, TOK, TOK), BF16),
        pltpu.VMEM((2, TOK, TOK), BF16),
        pltpu.VMEM((TOK, TOK), F32),
        pltpu.VMEM((2, TOK, STATE), BF16),
        pltpu.VMEM((2, STATE, TOK), BF16),
        pltpu.VMEM((FEAT // 128, 8, 128), F32),
        pltpu.VMEM((FEAT // 128, 8, 128), F32),
        pltpu.VMEM((FEAT // 128, 8, 128), F32),
        pltpu.VMEM((RING, 8, 128), F32),
        pltpu.VMEM((TOK, TOK), F32),
        pltpu.VMEM((1, FEAT), F32),
        pltpu.VMEM((8, FEAT), F32),
        pltpu.VMEM((TOK, 128), F32),
        state,
        state,
        message,
        message,
        message,
        message,
        state,
        state,
        state,
        state,
        pair,
        pair,
        pltpu.VMEM((TOK, 2 * STATE), F32),
        pltpu.VMEM((TOK, 2 * STATE), F32),
        pltpu.VMEM((HEADS_AX, quarter, 2 * STATE), F32),
        pltpu.VMEM((quarter, 2 * STATE), F32),
        pltpu.VMEM((HEADS_AX, quarter, 2 * STATE), F32),
        tile,
        tile,
        tile,
        pltpu.VMEM((RING, 8, 128), F32),
        tile,
        pltpu.VMEM((ROWS, 8, 128), F32),
        sems,
        sems,
        sems,
        sems,
        sems,
        sems,
        sems,
        sems,
        pltpu.SemaphoreType.DMA((HEADS_AX,)),
        pltpu.SemaphoreType.DMA((HEADS_AX,)),
        pltpu.SemaphoreType.DMA((HEADS_AX,)),
        pltpu.SemaphoreType.DMA((HEADS_AX,)),
        pltpu.SemaphoreType.DMA((RING + ROWS,)),
        pltpu.SemaphoreType.DMA((RING + ROWS,)),
        pltpu.SemaphoreType.DMA((RING,)),
        pltpu.SemaphoreType.DMA((RING,)),
    ]
    shapes = (
        jax.ShapeDtypeStruct((TOK, FEAT), BF16),
        jax.ShapeDtypeStruct((TOK, STATE), F32),
        jax.ShapeDtypeStruct((TOK, STATE), F32),
        jax.ShapeDtypeStruct((HEADS, TOK), F32),
        jax.ShapeDtypeStruct((1, HEADS), F32),
        jax.ShapeDtypeStruct((1, HEADS), F32),
    )
    results = pl.pallas_call(
        kernel,
        out_shape=shapes,
        in_specs=[vmem] * 8,
        out_specs=(vmem,) * 6,
        scratch_shapes=scratch,
        compiler_params=pltpu.CompilerParams(
            collective_id=0, has_side_effects=True, vmem_limit_bytes=56 << 20
        ),
    )(
        inputs[0],
        grad_out[0],
        proj_b[0],
        proj_c[0],
        step_size[0],
        decay_rate[None],
        skip_gain[None],
        doc_lengths,
    )
    grad_x, grad_b, grad_c, grad_step, grad_rate, grad_skip = pl.pallas_call(
        hand_out,
        out_shape=shapes,
        in_specs=[vmem] * 6,
        out_specs=(vmem,) * 6,
        compiler_params=pltpu.CompilerParams(vmem_limit_bytes=56 << 20),
    )(*results)
    return (
        grad_x[None],
        grad_b[None],
        grad_c[None],
        grad_step[None],
        grad_rate[0],
        grad_skip[0],
    )


def solution(mesh):
    in_specs = (
        P("dp", "seq", "head"),
        P("dp", "seq", None),
        P("dp", "seq", None),
        P("dp", "head", "seq"),
        P("head"),
        P("head"),
        P("dp", None),
        P("dp", "seq", "head"),
    )
    out_specs = (
        P("dp", "seq", "head"),
        P("dp", "seq", None),
        P("dp", "seq", None),
        P("dp", "head", "seq"),
        P("head"),
        P("head"),
    )
    return jax.shard_map(
        on_device, mesh=mesh, in_specs=in_specs, out_specs=out_specs, check_vma=False
    )
```

time: 120 us -> 101 us (0.84)
  Pallas kernels: 113 us -> 101 us
  local copies, waits for them, and re-layouts: 5.85 us -> 0 us
    pallas_call x1 -> x2, Pallas kernels: 113 us -> 101 us  [the longest x1 98.2 us: on_device(): pl.pallas_call(kernel, out_shape=shapes, in_specs=[vmem] * 8, out_specs=(...]
    unnamed x16 -> x0, local copies, waits for them, and re-layouts: 5.85 us -> none
where the time goes in v2:
time: 101 us
  Pallas kernels  101 us (100%)
    pallas_call x1, Pallas kernels, on_device(): pl.pallas_call(kernel, out_shape=shapes, in_specs=[vmem] * 8, out_specs=(...  98.2 us
    pallas_call x1, Pallas kernels, on_device(): pl.pallas_call(hand_out, out_shape=shapes, in_specs=[vmem] * 6, out_specs...  2.42 us

profile of v2, /device:TPU:8, one launch (start us, length us, event | category | flops | bytes accessed | tf_op | source)
XLA Modules:
  0.0 101.3 jit_solution(16651136146610311545)
XLA Ops:
  0.6 98.2 %shard_map.127 = (bf16[256,2048]{1,0:T(8,128)(2,1)}, f32[256,128]{1,0:T(8,128)}, f32[256,128]{1,0:T(8,128)}, f32[32,256]{1,0:T(8,128)}, f32[1,32]{1,0:T(1,128)}, /*index=5*/f32[1,32]{1,0:T(1,128)}) custom-call(bf16[256,2048]{1,0:T(8,128)(2,1)} %bitcast.13, bf16[256,2048]{1,0:T(8,128)(2,1)} %bitcast.14, bf16[256,128]{1,0:T(8,128)(2,1)} %bitcast.15, ...), custom_call_target="tpu_custom_call" | custom-call | tf_op jit(solution)/shard_map/pallas_call | solution.py:702
  98.9 2.4 %shard_map.128 = (bf16[256,2048]{1,0:T(8,128)(2,1)}, f32[256,128]{1,0:T(8,128)}, f32[256,128]{1,0:T(8,128)}, f32[32,256]{1,0:T(8,128)}, f32[1,32]{1,0:T(1,128)}, /*index=5*/f32[1,32]{1,0:T(1,128)}) custom-call(bf16[256,2048]{1,0:T(8,128)(2,1)} %get-tuple-element.18.refs_0_, f32[256,128]{1,0:T(8,128)} %get-tuple-element.19.refs_1_, ...), custom_call_target="tpu_custom_call" | custom-call | tf_op jit(solution)/shard_map/pallas_call | solution.py:721

commit v3 on v2

--- a/solution.py
+++ b/solution.py
@@ -25,11 +25,12 @@
 SLICES = PER * GROUPS
 HALF = STATE // PIECES
 LATE = SLICES // 2
-HOP = 3 * PIECES // 2
+HOP = 11 * PIECES // 2
 LAG = 3 * PIECES // 2
 DELAY = PER + 2
-SLOTS = HOP * (RING - 1) + SLICES
+SLOTS = HOP * (RING - 1) // 4 + SLICES
 ORDER = (0, 1, 4, 2, 5, 3, 6, 7)
+READY = 2
 
 
 def nn(a, b):
@@ -65,8 +66,8 @@
 
 
 def kernel(
-    x_ref,
-    dy_ref,
+    x_hbm,
+    dy_hbm,
     b_ref,
     c_ref,
     step_ref,
@@ -79,6 +80,8 @@
     gs_ref,
     gr_ref,
     gk_ref,
+    x_ref,
+    dy_ref,
     xh_ref,
     xl_ref,
     dyh_ref,
@@ -140,6 +143,7 @@
     v_recv,
     t_send,
     t_recv,
+    in_sems,
 ):
     core = lax.axis_index("dp")
     k = lax.axis_index("seq")
@@ -158,6 +162,11 @@
     barrier = pltpu.get_barrier_semaphore()
     for peer in peers:
         pl.semaphore_signal(barrier, inc=1, device_id=peer, device_id_type=MESH)
+
+    load_x = pltpu.make_async_copy(x_hbm, x_ref, in_sems.at[0])
+    load_dy = pltpu.make_async_copy(dy_hbm, dy_ref, in_sems.at[1])
+    load_x.start()
+    load_dy.start()
 
     lens = len_ref[...].astype(F32)
     docs = lens.shape[1]
@@ -189,7 +198,7 @@
     skip_col = jnp.sum(jnp.where(hsub == hlane, skip_ref[...], 0.0), axis=1, keepdims=True)
     step = step_ref[...]
     tri = jnp.where(rows >= cols, 1.0, 0.0).astype(BF16)
-    owner = jnp.where(iota((HEADS, FEAT), 1) // HEAD_DIM == iota((HEADS, FEAT), 0), 1.0, 0.0)
+    owner = jnp.where(over(iota((HEADS, FEAT), 1), HEAD_DIM) == iota((HEADS, FEAT), 0), 1.0, 0.0)
     ob_ref[...] = owner.astype(BF16)
     skx_ref[...] = jnp.sum(owner * skip_col, axis=0, keepdims=True)
     running = sum(nt(tri, part) for part in split3(-(step * rate_col)))
@@ -205,7 +214,6 @@
             device_id_type=MESH,
         )
 
-    pl.semaphore_wait(barrier, len(peers))
     passing = jnp.exp(running[TOK - 1 :, :]) * same_end
     wide = jnp.concatenate([passing, jnp.zeros((1, 128 - HEADS), F32)], axis=1)
     thz_ref[z] = jnp.broadcast_to(wide, (8, 128))
@@ -215,9 +223,6 @@
         return remote(
             thz_ref.at[z], thz_ref.at[slot], t_send.at[d], t_recv.at[d], {"seq": target}
         )
-
-    for d in range(1, RING):
-        copy_t(d, z).start()
 
     def prepare(i):
         at = pl.ds(pl.multiple_of(i * WIDE, WIDE), WIDE)
@@ -245,6 +250,23 @@
                 l_ref[PER * i + PIECES * q + n] = local[some, cut]
                 ld_ref[PER * i + PIECES * q + n] = local_d[some, cut]
 
+    def choose(place):
+        chosen = 0
+        for n in range(1, GROUPS):
+            chosen = jnp.where(place == n, ORDER[n], chosen)
+        return chosen
+
+    def prepare_next(place, _):
+        prepare(choose(place))
+        return 0
+
+    load_x.wait()
+    load_dy.wait()
+    lax.fori_loop(0, READY, prepare_next, 0)
+    pl.semaphore_wait(barrier, len(peers))
+    for d in range(1, RING):
+        copy_t(d, z).start()
+
     def make_weights():
         for d in range(1, RING):
             copy_t(d, lax.rem(z + RING - d, RING)).wait()
@@ -273,11 +295,23 @@
     rc_ref[...] = jnp.zeros_like(rc_ref)
     ds_ref[...] = jnp.zeros_like(ds_ref)
 
-    def copy_p(s):
-        return remote(send_p.at[s], recv_p.at[s], p_send.at[s], p_recv.at[s], {"seq": right})
-
-    def copy_m(s):
-        return remote(send_m.at[s], recv_m.at[s], m_send.at[s], m_recv.at[s], {"seq": left})
+    def copy_p(part, s):
+        return remote(
+            send_p.at[part, s],
+            recv_p.at[part, s],
+            p_send.at[part, s],
+            p_recv.at[part, s],
+            {"seq": right},
+        )
+
+    def copy_m(part, s):
+        return remote(
+            send_m.at[part, s],
+            recv_m.at[part, s],
+            m_send.at[part, s],
+            m_recv.at[part, s],
+            {"seq": left},
+        )
 
     def copy_s(s):
         return remote(ysend_s.at[s], cin_s.at[s], s_send.at[s], s_recv.at[s], {"seq": up})
@@ -289,31 +323,24 @@
         fb = over(s, PIECES)
         return th_ref[fb, 0:1], w_ref[fb, 0:1], w_ref[fb, 1:2], w_ref[fb, 2:3]
 
-    def chain(s, first, final, copy, recv, send, mine, other, cin_mine, cin_other, forward):
-        th, ahead, behind, _ = weights(s)
-        weight = ahead if forward else behind
-
+    def chain(part, s, first, final, copy, recv, send, make):
         @pl.when(first)
         def _():
-            recv[s] = jnp.zeros((2 * HALF, 128), F32)
+            recv[part, s] = jnp.zeros((HALF, 128), F32)
 
         @pl.when(jnp.logical_not(first))
         def _():
-            copy(s).wait_recv()
-
-        @pl.when(s < LATE)
-        def _():
-            send[s, :HALF] = th * recv[s, :HALF] + mine[s]
-            send[s, HALF:] = recv[s, HALF:] + weight * other[s]
-
-        @pl.when(s >= LATE)
-        def _():
-            send[s, :HALF] = th * (recv[s, :HALF] + weight * cin_mine[s]) + mine[s]
-            send[s, HALF:] = recv[s, HALF:] + cin_other[s]
+            copy(part, s).wait_recv()
+
+        for late in range(2):
+
+            @pl.when(s >= LATE if late else s < LATE)
+            def _():
+                send[part, s] = make(late, recv[part, s])
 
         @pl.when(jnp.logical_not(final))
         def _():
-            copy(s).start()
+            copy(part, s).start()
 
     def pass_on(s, has_recv, has_send, copy, cin, ysend, total):
         @pl.when(has_recv)
@@ -341,7 +368,7 @@
 
     def own_heads(i):
         shape = (WIDE, 128)
-        hit = iota(shape, 0) // HEAD_DIM + 4 * i == iota(shape, 1)
+        hit = over(iota(shape, 0), HEAD_DIM) + 4 * i == iota(shape, 1)
         return jnp.where(hit, 1.0, 0.0).astype(BF16)
 
     def add_products(i, at, y_part, dx_part, extra):
@@ -413,33 +440,44 @@
         whole = whole + skx_ref[:, at] * dy_ref[:, at].astype(F32)
         gx_ref[:, at] = whole.astype(BF16)
 
-    far = HOP * jnp.maximum(z, RING - 1 - z)
+    from_left = over(HOP * z, 4)
+    from_right = over(HOP * (RING - 1 - z), 4)
+    far = jnp.maximum(from_left, from_right)
+    need = jnp.where((z == 0) | (z == RING - 1), DELAY, over(HOP, 4))
     hops_s, hops_d = y, ROWS - 1 - y
 
-    def slot_body(number, _):
-        tau = number - 1
-
-        @pl.when(tau == 2)
-        def _():
-            make_weights()
-
+    def slot_body(tau, _):
         def at(n, low, high, work):
             @pl.when((n >= low) & (n < high))
             def _():
                 work(n)
 
-        def forward(s):
-            chain(
-                s, z == 0, z == RING - 1, copy_p, recv_p, send_p, l_ref, ld_ref, cin_s, cin_d, True
-            )
-
-        def backward(s):
-            chain(
-                s, z == RING - 1, z == 0, copy_m, recv_m, send_m, ld_ref, l_ref, cin_d, cin_s, False
-            )
-
-        at(tau - HOP * z, 0, SLICES, forward)
-        at(tau - HOP * (RING - 1 - z), 0, SLICES, backward)
+        def run(forward, part, s):
+            th, ahead, behind, _ = weights(s)
+            weight = ahead if forward else behind
+            mine, other = (l_ref, ld_ref) if forward else (ld_ref, l_ref)
+            cin_mine, cin_other = (cin_s, cin_d) if forward else (cin_d, cin_s)
+
+            def make(late, value):
+                if part:
+                    return value + (cin_other[s] if late else weight * other[s])
+                if late:
+                    value = value + weight * cin_mine[s]
+                return th * value + mine[s]
+
+            ends = (z == 0, z == RING - 1) if forward else (z == RING - 1, z == 0)
+            copy, recv, send = (copy_p, recv_p, send_p) if forward else (copy_m, recv_m, send_m)
+            chain(part, s, *ends, copy, recv, send, make)
+
+        at(tau - from_left, 0, SLICES, lambda s: run(True, 0, s))
+        at(tau - from_right, 0, SLICES, lambda s: run(False, 0, s))
+
+        @pl.when(tau == need)
+        def _():
+            make_weights()
+
+        at(tau - from_left, 0, SLICES, lambda s: run(True, 1, s))
+        at(tau - from_right, 0, SLICES, lambda s: run(False, 1, s))
 
         def early_s(s):
             pass_s(s, lambda s: weights(s)[2] * l_ref[s])
@@ -451,20 +489,20 @@
         at(tau + LATE - DELAY - LAG * hops_d, LATE, SLICES, early_d)
 
         def late_s(s):
-            pass_s(s, lambda s: weights(s)[2] * send_p[s, :HALF] + recv_m[s, HALF:])
-            keep(s, recv_p[s, :HALF] + weights(s)[1] * cin_s[s], cin_s, sp_ref)
+            pass_s(s, lambda s: weights(s)[2] * send_p[0, s] + recv_m[1, s])
+            keep(s, recv_p[0, s] + weights(s)[1] * cin_s[s], cin_s, sp_ref)
 
         def late_d(s):
-            pass_d(s, lambda s: weights(s)[1] * send_m[s, :HALF] + recv_p[s, HALF:])
-            keep(s, recv_m[s, :HALF] + weights(s)[2] * cin_d[s], cin_d, dp_ref)
+            pass_d(s, lambda s: weights(s)[1] * send_m[0, s] + recv_p[1, s])
+            keep(s, recv_m[0, s] + weights(s)[2] * cin_d[s], cin_d, dp_ref)
 
         at(tau - far - LAG * hops_s, 0, LATE, late_s)
         at(tau - far - LAG * hops_d, 0, LATE, late_d)
 
         def whole(s):
             _, ahead, behind, _ = weights(s)
-            state = recv_p[s, :HALF] + ahead * (cin_s[s] + recv_m[s, HALF:])
-            state_d = recv_m[s, :HALF] + behind * (cin_d[s] + recv_p[s, HALF:])
+            state = recv_p[0, s] + ahead * (cin_s[s] + recv_m[1, s])
+            state_d = recv_m[0, s] + behind * (cin_d[s] + recv_p[1, s])
             keep(s, state, cin_s, sp_ref)
             keep(s, state_d, cin_d, dp_ref)
 
@@ -475,14 +513,11 @@
             make_scores()
 
         beat = PER // 2
-        place = over(tau + beat, beat)
-
-        @pl.when((tau == -1) | ((left_over(tau + beat, beat) == 0) & (place < GROUPS)))
-        def _():
-            chosen = 0
-            for n in range(1, GROUPS):
-                chosen = jnp.where((tau >= 0) & (place == n), ORDER[n], chosen)
-            prepare(chosen)
+        place = over(tau, beat) + READY
+
+        @pl.when((left_over(tau, beat) == 0) & (place < GROUPS))
+        def _():
+            prepare(choose(place))
 
         turn = left_over(tau, PER)
 
@@ -505,38 +540,40 @@
         lax.fori_loop(0, 2, both, 0)
         return 0
 
-    lax.fori_loop(0, SLOTS + 1, slot_body, 0)
+    lax.fori_loop(0, SLOTS, slot_body, 0)
 
     d_scores = jnp.where(mask_ref[...] > 0.5, ds_ref[...], 0.0)
     bq, cq = b_ref[...], c_ref[...]
     sh, sl = split2(d_scores)
-    th, tl = split2(d_scores.T)
-    part_ref[:, :STATE] = leave * acc_ref[:, :STATE] + nn(th, cq) + nn(tl, cq)
-    part_ref[:, STATE:] = enter * acc_ref[:, STATE:] + nn(sh, bq) + nn(sl, bq)
     quarter = TOK // HEADS_AX
 
-    def copy_rs(d):
+    def copy_rs(n, d):
         target = lax.rem(head + d, HEADS_AX)
         rows_of = pl.ds(pl.multiple_of(target * quarter, quarter), quarter)
         return remote(
-            part_ref.at[rows_of], rs_ref.at[d], rs_send.at[d], rs_recv.at[d], {"head": target}
+            part_ref.at[n, rows_of],
+            rs_ref.at[n, d],
+            rs_send.at[n, d],
+            rs_recv.at[n, d],
+            {"head": target},
         )
 
-    def copy_ag(d):
-        target = lax.rem(head + d, HEADS_AX)
+    def copy_ag(n, d, slot):
         return remote(
-            sum_ref, full_ref.at[head], ag_send.at[d], ag_recv.at[d], {"head": target}
+            sum_ref.at[n],
+            full_ref.at[n, slot],
+            ag_send.at[n, d],
+            ag_recv.at[n, d],
+            {"head": lax.rem(head + d, HEADS_AX)},
         )
 
-    def wait_ag(d):
-        source = lax.rem(head + HEADS_AX - d, HEADS_AX)
-        target = lax.rem(head + d, HEADS_AX)
-        return remote(
-            sum_ref, full_ref.at[source], ag_send.at[d], ag_recv.at[d], {"head": target}
-        )
-
+    part_ref[1] = enter * acc_ref[:, STATE:] + nn(sh, bq) + nn(sl, bq)
     for d in range(1, HEADS_AX):
-        copy_rs(d).start()
+        copy_rs(1, d).start()
+    th, tl = split2(d_scores.T)
+    part_ref[0] = leave * acc_ref[:, :STATE] + nn(th, cq) + nn(tl, cq)
+    for d in range(1, HEADS_AX):
+        copy_rs(0, d).start()
 
     tri = jnp.where(iota((TOK, TOK), 0) >= iota((TOK, TOK), 1), 1.0, 0.0).astype(BF16)
     dl = sum(nn(part[:HEADS], tri) for part in split3(rc_ref[...].T))
@@ -562,12 +599,36 @@
     for d in range(1, RING):
         copy_z(d, z).start()
     mine_rows = pl.ds(pl.multiple_of(head * quarter, quarter), quarter)
-    for d in range(1, HEADS_AX):
-        copy_rs(d).wait()
-    sum_ref[...] = part_ref[mine_rows] + rs_ref[1] + rs_ref[2] + rs_ref[3]
-    full_ref[head] = sum_ref[...]
-    for d in range(1, HEADS_AX):
-        copy_ag(d).start()
+    def drain(s, _):
+        @pl.when(z < RING - 1)
+        def _():
+            copy_p(0, s).wait_send()
+            copy_p(1, s).wait_send()
+
+        @pl.when(z > 0)
+        def _():
+            copy_m(0, s).wait_send()
+            copy_m(1, s).wait_send()
+
+        @pl.when(y < ROWS - 1)
+        def _():
+            copy_s(s).wait_send()
+
+        @pl.when(y > 0)
+        def _():
+            copy_d(s).wait_send()
+
+        return 0
+
+    lax.fori_loop(0, SLICES, drain, 0)
+
+    for n in (1, 0):
+        for d in range(1, HEADS_AX):
+            copy_rs(n, d).wait()
+        sum_ref[n] = part_ref[n, mine_rows] + rs_ref[n, 1] + rs_ref[n, 2] + rs_ref[n, 3]
+        full_ref[n, head] = sum_ref[n]
+        for d in range(1, HEADS_AX):
+            copy_ag(n, d, head).start()
 
     for d in range(1, RING):
         copy_z(d, lax.rem(z + RING - d, RING)).wait()
@@ -581,54 +642,52 @@
 
     for d in range(1, ROWS):
         copy_y(d, y).start()
-    for d in range(1, HEADS_AX):
-        wait_ag(d).wait()
-    for n in range(HEADS_AX):
-        gb_ref[n * quarter : (n + 1) * quarter] = full_ref[n, :, :STATE]
-        gc_ref[n * quarter : (n + 1) * quarter] = full_ref[n, :, STATE:]
+    for n, out_ref in ((1, gc_ref), (0, gb_ref)):
+        for d in range(1, HEADS_AX):
+            copy_ag(n, d, lax.rem(head + HEADS_AX - d, HEADS_AX)).wait()
+        for m in range(HEADS_AX):
+            out_ref[m * quarter : (m + 1) * quarter] = full_ref[n, m]
     for d in range(1, ROWS):
         copy_y(d, lax.rem(y + ROWS - d, ROWS)).wait()
     whole_vec = sum(vy_ref[n] for n in range(ROWS))
     gr_ref[...] = whole_vec[0:1, :HEADS]
     gk_ref[...] = whole_vec[1:2, :HEADS]
 
-    def drain(s, _):
-        @pl.when(z < RING - 1)
-        def _():
-            copy_p(s).wait_send()
-
-        @pl.when(z > 0)
-        def _():
-            copy_m(s).wait_send()
-
-        @pl.when(y < ROWS - 1)
-        def _():
-            copy_s(s).wait_send()
-
-        @pl.when(y > 0)
-        def _():
-            copy_d(s).wait_send()
-
-        return 0
-
-    lax.fori_loop(0, SLICES, drain, 0)
-
 
 def hand_out(*refs):
-    count = len(refs) // 2
-    for n in range(count):
-        refs[count + n][...] = refs[n][...]
+    ins, outs, held, sems_in, sems_out = refs[:6], refs[6:12], refs[12:18], refs[18], refs[19]
+    pieces = [(n, None) for n in range(1, 6)]
+    pieces = [(0, pl.ds(m * TOK // 4, TOK // 4)) for m in range(4)] + pieces
+
+    def cut(ref, rows):
+        return ref if rows is None else ref.at[rows]
+
+    loads, stores = [], []
+    for m, (n, rows) in enumerate(pieces):
+        there, here, out = cut(ins[n], rows), cut(held[n], rows), cut(outs[n], rows)
+        loads.append(pltpu.make_async_copy(there, here, sems_in.at[m]))
+        stores.append(pltpu.make_async_copy(here, out, sems_out.at[m]))
+    for load in loads:
+        load.start()
+    for load, store in zip(loads, stores):
+        load.wait()
+        store.start()
+    for store in stores:
+        store.wait()
 
 
 def on_device(inputs, proj_b, proj_c, step_size, decay_rate, skip_gain, doc_lengths, grad_out):
     vmem = pl.BlockSpec(memory_space=pltpu.VMEM)
     state = pltpu.VMEM((SLICES, HALF, 128), F32)
-    message = pltpu.VMEM((SLICES, 2 * HALF, 128), F32)
+    message = pltpu.VMEM((2, SLICES, HALF, 128), F32)
     pair = pltpu.VMEM((2, SLICES, HALF, 128), BF16)
     sems = pltpu.SemaphoreType.DMA((SLICES,))
+    both = pltpu.SemaphoreType.DMA((2, SLICES))
     tile = pltpu.VMEM((8, 128), F32)
     quarter = TOK // HEADS_AX
     scratch = [
+        pltpu.VMEM((TOK, FEAT), BF16),
+        pltpu.VMEM((TOK, FEAT), BF16),
         pltpu.VMEM((TOK, FEAT), BF16),
         pltpu.VMEM((TOK, FEAT), BF16),
         pltpu.VMEM((TOK, FEAT), BF16),
@@ -664,32 +723,33 @@
         pair,
         pair,
         pltpu.VMEM((TOK, 2 * STATE), F32),
-        pltpu.VMEM((TOK, 2 * STATE), F32),
-        pltpu.VMEM((HEADS_AX, quarter, 2 * STATE), F32),
-        pltpu.VMEM((quarter, 2 * STATE), F32),
-        pltpu.VMEM((HEADS_AX, quarter, 2 * STATE), F32),
+        pltpu.VMEM((2, TOK, STATE), F32),
+        pltpu.VMEM((2, HEADS_AX, quarter, STATE), F32),
+        pltpu.VMEM((2, quarter, STATE), F32),
+        pltpu.VMEM((2, HEADS_AX, quarter, STATE), F32),
         tile,
         tile,
         tile,
         pltpu.VMEM((RING, 8, 128), F32),
         tile,
         pltpu.VMEM((ROWS, 8, 128), F32),
+        both,
+        both,
+        both,
+        both,
         sems,
         sems,
         sems,
         sems,
-        sems,
-        sems,
-        sems,
-        sems,
-        pltpu.SemaphoreType.DMA((HEADS_AX,)),
-        pltpu.SemaphoreType.DMA((HEADS_AX,)),
-        pltpu.SemaphoreType.DMA((HEADS_AX,)),
-        pltpu.SemaphoreType.DMA((HEADS_AX,)),
+        pltpu.SemaphoreType.DMA((2, HEADS_AX)),
+        pltpu.SemaphoreType.DMA((2, HEADS_AX)),
+        pltpu.SemaphoreType.DMA((2, HEADS_AX)),
+        pltpu.SemaphoreType.DMA((2, HEADS_AX)),
         pltpu.SemaphoreType.DMA((RING + ROWS,)),
         pltpu.SemaphoreType.DMA((RING + ROWS,)),
         pltpu.SemaphoreType.DMA((RING,)),
         pltpu.SemaphoreType.DMA((RING,)),
+        pltpu.SemaphoreType.DMA((2,)),
     ]
     shapes = (
         jax.ShapeDtypeStruct((TOK, FEAT), BF16),
@@ -699,10 +759,11 @@
         jax.ShapeDtypeStruct((1, HEADS), F32),
         jax.ShapeDtypeStruct((1, HEADS), F32),
     )
+    anywhere = pl.BlockSpec(memory_space=pl.ANY)
     results = pl.pallas_call(
         kernel,
         out_shape=shapes,
-        in_specs=[vmem] * 8,
+        in_specs=[anywhere] * 2 + [vmem] * 6,
         out_specs=(vmem,) * 6,
         scratch_shapes=scratch,
         compiler_params=pltpu.CompilerParams(
@@ -721,8 +782,10 @@
     grad_x, grad_b, grad_c, grad_step, grad_rate, grad_skip = pl.pallas_call(
         hand_out,
         out_shape=shapes,
-        in_specs=[vmem] * 6,
-        out_specs=(vmem,) * 6,
+        in_specs=[anywhere] * 6,
+        out_specs=(anywhere,) * 6,
+        scratch_shapes=[pltpu.VMEM(shape.shape, shape.dtype) for shape in shapes]
+        + [pltpu.SemaphoreType.DMA((9,)), pltpu.SemaphoreType.DMA((9,))],
         compiler_params=pltpu.CompilerParams(vmem_limit_bytes=56 << 20),
     )(*results)
     return (

time: 101 us -> 98.1 us (0.971)
  Pallas kernels: 101 us -> 97.3 us
    pallas_call x2, Pallas kernels: 101 us -> 97.3 us  [the longest x1 95.1 us: on_device(): pl.pallas_call(kernel, out_shape=shapes, in_specs=[anywhere] * 2 + [vmem]...]
where the time goes in v3:
time: 98.1 us; the launch traced here: 97.9 us
  Pallas kernels  97.3 us (99%)
    pallas_call x1, Pallas kernels, on_device(): pl.pallas_call(kernel, out_shape=shapes, in_specs=[anywhere] * 2 + [vmem]...  95.1 us
    pallas_call x1, Pallas kernels, on_device(): pl.pallas_call(hand_out, out_shape=shapes, in_specs=[anywhere] * 6, out_s...  2.16 us

profile of v3, /device:TPU:8, one launch (start us, length us, event | category | flops | bytes accessed | tf_op | source)
XLA Modules:
  0.0 97.9 jit_solution(918674988390026171)
XLA Ops:
  0.6 95.1 %shard_map.127 = (bf16[256,2048]{1,0:T(8,128)(2,1)}, f32[256,128]{1,0:T(8,128)}, f32[256,128]{1,0:T(8,128)}, f32[32,256]{1,0:T(8,128)}, f32[1,32]{1,0:T(1,128)}, /*index=5*/f32[1,32]{1,0:T(1,128)}) custom-call(bf16[256,2048]{1,0:T(8,128)(2,1)} %bitcast.13, bf16[256,2048]{1,0:T(8,128)(2,1)} %bitcast.14, bf16[256,128]{1,0:T(8,128)(2,1)} %bitcast.15, ...), custom_call_target="tpu_custom_call" | custom-call | tf_op jit(solution)/shard_map/pallas_call | solution.py:763
  95.7 2.2 %shard_map.128 = (bf16[256,2048]{1,0:T(8,128)(2,1)}, f32[256,128]{1,0:T(8,128)}, f32[256,128]{1,0:T(8,128)}, f32[32,256]{1,0:T(8,128)}, f32[1,32]{1,0:T(1,128)}, /*index=5*/f32[1,32]{1,0:T(1,128)}) custom-call(bf16[256,2048]{1,0:T(8,128)(2,1)} %get-tuple-element.18.refs_0_, f32[256,128]{1,0:T(8,128)} %get-tuple-element.19.refs_1_, ...), custom_call_target="tpu_custom_call" | custom-call | tf_op jit(solution)/shard_map/pallas_call | solution.py:782

commit v4 on v3

--- a/solution.py
+++ b/solution.py
@@ -30,7 +30,7 @@
 DELAY = PER + 2
 SLOTS = HOP * (RING - 1) // 4 + SLICES
 ORDER = (0, 1, 4, 2, 5, 3, 6, 7)
-READY = 2
+READY = 1
 
 
 def nn(a, b):
@@ -101,6 +101,7 @@
     w_ref,
     thz_ref,
     mask_ref,
+    skr_ref,
     skx_ref,
     sk_ref,
     rc_ref,
@@ -508,7 +509,7 @@
 
         at(tau - far, LATE, SLICES, whole)
 
-        @pl.when(tau == 0)
+        @pl.when(tau == 1)
         def _():
             make_scores()
 
@@ -518,6 +519,21 @@
         @pl.when((left_over(tau, beat) == 0) & (place < GROUPS))
         def _():
             prepare(choose(place))
+
+        @pl.when(tau == SLICES + PER)
+        def _():
+            d_scores = jnp.where(mask_ref[...] > 0.5, ds_ref[...], 0.0)
+            sh, sl = split2(d_scores)
+            part_ref[1] = nn(sh, b_ref[...]) + nn(sl, b_ref[...])
+            th, tl = split2(d_scores.T)
+            part_ref[0] = nn(th, c_ref[...]) + nn(tl, c_ref[...])
+
+        @pl.when(tau == SLICES + PER + 1)
+        def _():
+            skip_part = sum(nt(ob_ref[...], part) for part in split3(sk_ref[...]))[:, :1]
+            diag = iota((HEADS, 128), 0) == iota((HEADS, 128), 1)
+            skip_row = jnp.sum(jnp.where(diag, skip_part, 0.0), axis=0, keepdims=True)
+            skr_ref[...] = jnp.broadcast_to(skip_row, (8, 128))
 
         turn = left_over(tau, PER)
 
@@ -542,9 +558,6 @@
 
     lax.fori_loop(0, SLOTS, slot_body, 0)
 
-    d_scores = jnp.where(mask_ref[...] > 0.5, ds_ref[...], 0.0)
-    bq, cq = b_ref[...], c_ref[...]
-    sh, sl = split2(d_scores)
     quarter = TOK // HEADS_AX
 
     def copy_rs(n, d):
@@ -567,11 +580,10 @@
             {"head": lax.rem(head + d, HEADS_AX)},
         )
 
-    part_ref[1] = enter * acc_ref[:, STATE:] + nn(sh, bq) + nn(sl, bq)
+    part_ref[1] += enter * acc_ref[:, STATE:]
     for d in range(1, HEADS_AX):
         copy_rs(1, d).start()
-    th, tl = split2(d_scores.T)
-    part_ref[0] = leave * acc_ref[:, :STATE] + nn(th, cq) + nn(tl, cq)
+    part_ref[0] += leave * acc_ref[:, :STATE]
     for d in range(1, HEADS_AX):
         copy_rs(0, d).start()
 
@@ -579,12 +591,10 @@
     dl = sum(nn(part[:HEADS], tri) for part in split3(rc_ref[...].T))
     gs_ref[...] = -(rate_col * dl)
     rate_part = -jnp.sum(step * dl, axis=1, keepdims=True)
-    skip_part = sum(nt(ob_ref[...], part) for part in split3(sk_ref[...]))[:, :1]
     diag = iota((HEADS, 128), 0) == iota((HEADS, 128), 1)
     rate_row = jnp.sum(jnp.where(diag, rate_part, 0.0), axis=0, keepdims=True)
-    skip_row = jnp.sum(jnp.where(diag, skip_part, 0.0), axis=0, keepdims=True)
     first = iota((8, 128), 0)
-    vec_ref[...] = jnp.where(first == 0, rate_row, jnp.where(first == 1, skip_row, 0.0))
+    vec_ref[...] = jnp.where(first == 0, rate_row, jnp.where(first == 1, skr_ref[...], 0.0))
 
     swap = remote(vec_ref, vdp_ref, v_send.at[0], v_recv.at[0], {"dp": 1 - core})
     swap.start()
@@ -707,6 +717,7 @@
         pltpu.VMEM((FEAT // 128, 8, 128), F32),
         pltpu.VMEM((RING, 8, 128), F32),
         pltpu.VMEM((TOK, TOK), F32),
+        tile,
         pltpu.VMEM((1, FEAT), F32),
         pltpu.VMEM((8, FEAT), F32),
         pltpu.VMEM((TOK, 128), F32),

time: 98.1 us -> 97.7 us (level)
  no operation moved by 1% of the time
where the time goes in v4:
time: 97.7 us; the launch traced here: 97.5 us
  Pallas kernels  96.8 us (99%)
    pallas_call x1, Pallas kernels, on_device(): pl.pallas_call(kernel, out_shape=shapes, in_specs=[anywhere] * 2 + [vmem]...  94.7 us
    pallas_call x1, Pallas kernels, on_device(): pl.pallas_call(hand_out, out_shape=shapes, in_specs=[anywhere] * 6, out_s...  2.16 us

profile of v4, /device:TPU:8, one launch (start us, length us, event | category | flops | bytes accessed | tf_op | source)
XLA Modules:
  0.0 97.5 jit_solution(15325506776612134333)
XLA Ops:
  0.6 94.7 %shard_map.127 = (bf16[256,2048]{1,0:T(8,128)(2,1)}, f32[256,128]{1,0:T(8,128)}, f32[256,128]{1,0:T(8,128)}, f32[32,256]{1,0:T(8,128)}, f32[1,32]{1,0:T(1,128)}, /*index=5*/f32[1,32]{1,0:T(1,128)}) custom-call(bf16[256,2048]{1,0:T(8,128)(2,1)} %bitcast.13, bf16[256,2048]{1,0:T(8,128)(2,1)} %bitcast.14, bf16[256,128]{1,0:T(8,128)(2,1)} %bitcast.15, ...), custom_call_target="tpu_custom_call" | custom-call | tf_op jit(solution)/shard_map/pallas_call | solution.py:774
  95.3 2.2 %shard_map.128 = (bf16[256,2048]{1,0:T(8,128)(2,1)}, f32[256,128]{1,0:T(8,128)}, f32[256,128]{1,0:T(8,128)}, f32[32,256]{1,0:T(8,128)}, f32[1,32]{1,0:T(1,128)}, /*index=5*/f32[1,32]{1,0:T(1,128)}) custom-call(bf16[256,2048]{1,0:T(8,128)(2,1)} %get-tuple-element.18.refs_0_, f32[256,128]{1,0:T(8,128)} %get-tuple-element.19.refs_1_, ...), custom_call_target="tpu_custom_call" | custom-call | tf_op jit(solution)/shard_map/pallas_call | solution.py:793

commit v5 on v4

--- a/solution.py
+++ b/solution.py
@@ -160,14 +160,13 @@
     peers += [{"seq": y * RING + lax.rem(z + d, RING)} for d in range(1, RING)]
     peers += [{"seq": lax.rem(y + d, ROWS) * RING + z} for d in range(1, ROWS)]
     peers += [{"head": lax.rem(head + d, HEADS_AX)} for d in range(1, HEADS_AX)]
-    barrier = pltpu.get_barrier_semaphore()
-    for peer in peers:
-        pl.semaphore_signal(barrier, inc=1, device_id=peer, device_id_type=MESH)
-
     load_x = pltpu.make_async_copy(x_hbm, x_ref, in_sems.at[0])
     load_dy = pltpu.make_async_copy(dy_hbm, dy_ref, in_sems.at[1])
     load_x.start()
     load_dy.start()
+    barrier = pltpu.get_barrier_semaphore()
+    for peer in peers:
+        pl.semaphore_signal(barrier, inc=1, device_id=peer, device_id_type=MESH)
 
     lens = len_ref[...].astype(F32)
     docs = lens.shape[1]

time: 97.7 us -> 97.7 us (level)
  no operation moved by 1% of the time
where the time goes in v5:
time: 97.7 us; the launch traced here: 97.5 us
  Pallas kernels  96.9 us (99%)
    pallas_call x1, Pallas kernels, on_device(): pl.pallas_call(kernel, out_shape=shapes, in_specs=[anywhere] * 2 + [vmem]...  94.7 us
    pallas_call x1, Pallas kernels, on_device(): pl.pallas_call(hand_out, out_shape=shapes, in_specs=[anywhere] * 6, out_s...  2.16 us

profile of v5, /device:TPU:8, one launch (start us, length us, event | category | flops | bytes accessed | tf_op | source)
XLA Modules:
  0.0 97.5 jit_solution(6674426452425922811)
XLA Ops:
  0.6 94.7 %shard_map.127 = (bf16[256,2048]{1,0:T(8,128)(2,1)}, f32[256,128]{1,0:T(8,128)}, f32[256,128]{1,0:T(8,128)}, f32[32,256]{1,0:T(8,128)}, f32[1,32]{1,0:T(1,128)}, /*index=5*/f32[1,32]{1,0:T(1,128)}) custom-call(bf16[256,2048]{1,0:T(8,128)(2,1)} %bitcast.13, bf16[256,2048]{1,0:T(8,128)(2,1)} %bitcast.14, bf16[256,128]{1,0:T(8,128)(2,1)} %bitcast.15, ...), custom_call_target="tpu_custom_call" | custom-call | tf_op jit(solution)/shard_map/pallas_call | solution.py:773
  95.4 2.2 %shard_map.128 = (bf16[256,2048]{1,0:T(8,128)(2,1)}, f32[256,128]{1,0:T(8,128)}, f32[256,128]{1,0:T(8,128)}, f32[32,256]{1,0:T(8,128)}, f32[1,32]{1,0:T(1,128)}, /*index=5*/f32[1,32]{1,0:T(1,128)}) custom-call(bf16[256,2048]{1,0:T(8,128)(2,1)} %get-tuple-element.18.refs_0_, f32[256,128]{1,0:T(8,128)} %get-tuple-element.19.refs_1_, ...), custom_call_target="tpu_custom_call" | custom-call | tf_op jit(solution)/shard_map/pallas_call | solution.py:792
